TPU v7x, 32 devices: a whole 2x2x4 slice. The times are simulated.
32 devices in a mesh: section: 2 (over core), dp: 16 (over z, y, x).
Axes of the slice: x: 2, y: 2, z: 4, core: 2. Of those that a mesh axis runs over, the one named last changes fastest.
Arguments:
- tokens: bfloat16 [2, 1024, 768], P(None, 'dp'), may hold values from -6 to 6
- out_grad: bfloat16 [2, 1024, 768], P(None, 'dp'), may hold values from -6 to 6
- routes: int32 [2, 2, 1024, 1], P('section', None, 'dp'), may hold values from 0 to 3; in each aligned block of 64 rows (0 to 63, 64 to 127, ..., all dimensions but the last counted through in order) at most 24 rows name the same one
- doc_lengths: int32 [2, 16, 2], P(None, 'dp'), may hold values from 1 to 48, 64 in all within a row
- norm_attn: bfloat16 [2, 768], P('section', 'dp'), may hold values from 0.25 to 1.75
- attn_qkv: bfloat16 [2, 768, 2304], P('section', 'dp'), may hold values from -0.21875 to 0.21875
- rel_bias: bfloat16 [2, 384], P('section', 'dp'), may hold values from -4 to 4
- attn_out: bfloat16 [2, 768, 768], P('section', 'dp'), may hold values from -0.875 to 0.875
- norm_ffn: bfloat16 [2, 768], P('section', 'dp'), may hold values from 0.25 to 1.75
- router: bfloat16 [2, 768, 4], P('section', 'dp'), may hold values from -0.109375 to 0.109375
- expert_in: bfloat16 [2, 16, 768, 768], P('section', 'dp'), may hold values from -0.21875 to 0.21875
- expert_out: bfloat16 [2, 16, 768, 768], P('section', 'dp'), may hold values from -0.4375 to 0.4375
Outputs:
- layer_outputs: bfloat16 [2, 2, 1024, 768], P('section', None, 'dp')
- layer_input_grads: float32 [2, 2, 1024, 768], P('section', None, 'dp')
- grad_norm_attn: float32 [2, 768], P('section', 'dp')
- grad_attn_qkv: float32 [2, 768, 2304], P('section', 'dp')
- grad_rel_bias: float32 [2, 384], P('section', 'dp')
- grad_attn_out: float32 [2, 768, 768], P('section', 'dp')
- grad_norm_ffn: float32 [2, 768], P('section', 'dp')
- grad_router: float32 [2, 768, 4], P('section', 'dp')
- grad_expert_in: float32 [2, 16, 768, 768], P('section', 'dp')
- grad_expert_out: float32 [2, 16, 768, 768], P('section', 'dp')
Inputs may be any that keep to these rules, and one draw needn't show every extreme that they name: `routes`: in each layer and micro-batch the 64 rows of one device name each expert at most 24 times, a bound that some block reaches. `doc_lengths`: the 2 lengths of one device's share of a micro-batch sum to 64; neither is more than 48.
All inputs are finite; a program needn't handle non-finite values.
Results may differ from a plain program's by a relative error of at most 0.028.
Values may be sent and summed in bfloat16 or wider, within the bound.
A program may use at most 128 MiB of HBM per device.

v0:
```python
import math

import jax
import jax.numpy as jnp
import numpy as np
from jax import lax
from jax.sharding import PartitionSpec as P

HEADS = 12
HD = 64
BUCKETS = 32
SPLIT = 4


EPSILON = 1e-06
far_limits = np.array([8, 12, 16, 23, 32, 46, 64, 91], dtype=np.int32)


def shifted(block, axis, distance):
    devices = range(lax.axis_size(axis))
    route = [(i - distance, i) for i in devices if i - distance in devices]
    return lax.ppermute(block, axis, route)


def buckets_of(row_count):
    places = jnp.arange(row_count, dtype=jnp.int32)
    offset = places[None, :] - places[:, None]
    distance = jnp.abs(offset)
    beyond = jnp.sum(
        (distance[:, :, None] >= jnp.asarray(far_limits)[None, None, :]).astype(jnp.int32), axis=-1
    )
    nearby = jnp.where(distance < 8, distance, 7 + beyond)
    upward = jnp.where(offset > 0, BUCKETS // 2, 0).astype(jnp.int32)
    return nearby + upward


def documents_of(lengths, row_count):
    ending = jnp.cumsum(lengths, axis=-1)
    places = jnp.arange(row_count, dtype=jnp.int32)
    return jnp.sum((places[:, None] >= ending[..., None, :]).astype(jnp.int32), axis=-1)


def same_of(lengths, row_count):
    documents = documents_of(lengths, row_count)
    return documents[:, None] == documents[None, :]


def bias_of(table, row_count):
    bucket_picks = (
        buckets_of(row_count)[:, :, None] == jnp.arange(BUCKETS, dtype=jnp.int32)[None, None, :]
    ).astype(jnp.bfloat16)
    score_bias = jnp.einsum(
        "tsb,bh->hts",
        bucket_picks,
        table.reshape(BUCKETS, HEADS),
        preferred_element_type=jnp.float32,
    )
    return (score_bias, bucket_picks)


def split_heads(qkv_rows):
    row_count = qkv_rows.shape[0]
    model_width = qkv_rows.shape[1] // 3
    query_heads = qkv_rows[:, :model_width].reshape(row_count, HEADS, HD)
    key_heads = qkv_rows[:, model_width : 2 * model_width].reshape(row_count, HEADS, HD)
    value_heads = qkv_rows[:, 2 * model_width :].reshape(row_count, HEADS, HD)
    return (query_heads, key_heads, value_heads)


def scores_of(query_heads, key_heads, score_bias, same_doc):
    raw_scores = (
        jnp.einsum("thd,shd->hts", query_heads, key_heads, preferred_element_type=jnp.float32)
        * (1.0 / math.sqrt(HD))
        + score_bias
    )
    return jnp.where(same_doc[None], raw_scores, -1000000000.0)


def placement_of(route_now, expert_count, slot_count):
    row_count = route_now.shape[0]
    picked = (route_now[:, None] == jnp.arange(expert_count, dtype=jnp.int32)[None, :]).astype(
        jnp.int32
    )
    ranks = jnp.sum((jnp.cumsum(picked, axis=0) - 1) * picked, axis=1)
    target = route_now * slot_count + ranks
    flat = (
        jnp.arange(expert_count * slot_count, dtype=jnp.int32)[:, None] == target[None, :]
    ).astype(jnp.bfloat16)
    return flat.reshape(expert_count, slot_count, row_count)


def spread_copies(select, token_rows, dp_count):
    expert_count = select.shape[0]
    slot_count = select.shape[1]
    model_width = token_rows.shape[1]
    grouped = jnp.einsum(
        "ect,td->ecd", select, token_rows, preferred_element_type=jnp.float32
    ).astype(jnp.bfloat16)
    copies = jnp.broadcast_to(grouped[:, None], (expert_count, SPLIT, slot_count, model_width))
    return copies.reshape(dp_count, slot_count, model_width)


def rms_back(grad_rows, inputs, scale_rows):
    normal_rows = inputs * scale_rows
    return scale_rows * (
        grad_rows - normal_rows * jnp.mean(grad_rows * normal_rows, axis=-1, keepdims=True)
    )


def smooth(values):
    return jax.nn.gelu(values, approximate=True)


def layer_forward(layer_in, weights, route_now, lengths, weight_in, weight_back):
    gain_one, w_qkv, table, w_out, gain_two, w_route = weights
    row_count, model_width = layer_in.shape
    dp_count = lax.axis_size("dp")
    expert_count = w_route.shape[1]
    slot_count = 3 * row_count * SPLIT // (2 * dp_count)
    scale_one = lax.rsqrt(jnp.mean(layer_in * layer_in, axis=-1, keepdims=True) + EPSILON)
    normed = (layer_in * scale_one * gain_one.astype(jnp.float32)).astype(jnp.bfloat16)
    qkv_rows = jnp.dot(normed, w_qkv, preferred_element_type=jnp.float32).astype(jnp.bfloat16)
    query_heads, key_heads, value_heads = split_heads(qkv_rows)
    score_bias, bucket_picks = bias_of(table, row_count)
    same_doc = same_of(lengths, row_count)
    scores = scores_of(query_heads, key_heads, score_bias, same_doc)
    row_max = jnp.max(scores, axis=-1, keepdims=True)
    exp_rows = jnp.exp(scores - row_max)
    exp_total = jnp.sum(exp_rows, axis=-1, keepdims=True)
    log_total = row_max + jnp.log(exp_total)
    soft_low = (exp_rows / exp_total).astype(jnp.bfloat16)
    attended = jnp.einsum("hts,shd->thd", soft_low, value_heads, preferred_element_type=jnp.float32)
    attended = attended.reshape(row_count, model_width).astype(jnp.bfloat16)
    middle = layer_in + jnp.dot(attended, w_out, preferred_element_type=jnp.float32)
    scale_two = lax.rsqrt(jnp.mean(middle * middle, axis=-1, keepdims=True) + EPSILON)
    routed = (middle * scale_two * gain_two.astype(jnp.float32)).astype(jnp.bfloat16)
    logits = jnp.dot(routed, w_route, preferred_element_type=jnp.float32)
    choice_prob = jax.nn.softmax(logits, axis=-1)
    picked = (route_now[:, None] == jnp.arange(expert_count, dtype=jnp.int32)[None, :]).astype(
        jnp.float32
    )
    gate_prob = jnp.sum(choice_prob * picked, axis=-1)
    select = placement_of(route_now, expert_count, slot_count)
    outgoing = spread_copies(select, routed, dp_count)
    arrived = lax.all_to_all(outgoing, "dp", split_axis=0, concat_axis=0, tiled=True)
    token_rows = arrived.reshape(-1, model_width)
    hidden = jnp.dot(token_rows, weight_in, preferred_element_type=jnp.float32)
    active = smooth(hidden).astype(jnp.bfloat16)
    partial_out = (
        jnp.dot(active, weight_back, preferred_element_type=jnp.float32)
        .astype(jnp.bfloat16)
        .reshape(arrived.shape)
    )
    coming_back = lax.all_to_all(partial_out, "dp", split_axis=0, concat_axis=0, tiled=True)
    returned, hidden, arrived = (
        coming_back,
        hidden.reshape(arrived.shape[0], arrived.shape[1], -1),
        arrived,
    )
    combined = jnp.einsum(
        "ekcd,ect->td",
        returned.reshape(expert_count, SPLIT, slot_count, model_width),
        select,
        preferred_element_type=jnp.float32,
    )
    result = middle + gate_prob[:, None] * combined
    kept_state = (
        layer_in,
        scale_one,
        normed,
        qkv_rows,
        log_total,
        attended,
        middle,
        scale_two,
        routed,
        choice_prob,
        gate_prob,
        combined,
        hidden,
        arrived,
    )
    return (result, kept_state)


def layer_backward(upstream, kept_state, weights, route_now, lengths, weight_in, weight_back):
    (
        layer_in,
        scale_one,
        normed,
        qkv_rows,
        log_total,
        attended,
        middle,
        scale_two,
        routed,
        choice_prob,
        gate_prob,
        combined,
        hidden,
        arrived,
    ) = kept_state
    gain_one, w_qkv, table, w_out, gain_two, w_route = weights
    row_count, model_width = layer_in.shape
    dp_count = lax.axis_size("dp")
    expert_count = w_route.shape[1]
    slot_count = 3 * row_count * SPLIT // (2 * dp_count)
    picked = (route_now[:, None] == jnp.arange(expert_count, dtype=jnp.int32)[None, :]).astype(
        jnp.float32
    )
    select = placement_of(route_now, expert_count, slot_count)
    down_grad = (gate_prob[:, None] * upstream).astype(jnp.bfloat16)
    gate_grad = jnp.sum(upstream * combined, axis=-1)
    logit_grad = (choice_prob * (picked - gate_prob[:, None]) * gate_grad[:, None]).astype(
        jnp.bfloat16
    )
    routed_grad = jnp.einsum("te,de->td", logit_grad, w_route, preferred_element_type=jnp.float32)
    outgoing = spread_copies(select, down_grad, dp_count)
    arrived_grad = lax.all_to_all(outgoing, "dp", split_axis=0, concat_axis=0, tiled=True)
    rows_grad = arrived_grad.reshape(-1, model_width)
    active_grad = jnp.einsum(
        "rd,fd->rf", rows_grad, weight_back, preferred_element_type=jnp.float32
    )
    hidden_rows = hidden.reshape(rows_grad.shape[0], -1)
    active_rows, smooth_pull = jax.vjp(smooth, hidden_rows)
    hidden_grad = smooth_pull(active_grad)[0].astype(jnp.bfloat16)
    active_low = active_rows.astype(jnp.bfloat16)
    arrived_rows = arrived.reshape(-1, model_width)
    copy_grad = jnp.einsum(
        "rf,df->rd", hidden_grad, weight_in, preferred_element_type=jnp.float32
    ).astype(jnp.bfloat16)
    copy_back = lax.all_to_all(
        copy_grad.reshape(dp_count, slot_count, model_width),
        "dp",
        split_axis=0,
        concat_axis=0,
        tiled=True,
    )
    routed_grad = routed_grad + jnp.einsum(
        "ekcd,ect->td",
        copy_back.reshape(expert_count, SPLIT, slot_count, model_width),
        select,
        preferred_element_type=jnp.float32,
    )
    gain_two_grad = jnp.sum(routed_grad * middle * scale_two, axis=0)
    middle_grad = upstream + rms_back(routed_grad * gain_two.astype(jnp.float32), middle, scale_two)
    branch_grad = middle_grad.astype(jnp.bfloat16)
    attended_grad = jnp.einsum(
        "te,de->td", branch_grad, w_out, preferred_element_type=jnp.float32
    ).astype(jnp.bfloat16)
    attended_grad = attended_grad.reshape(row_count, HEADS, HD)
    query_heads, key_heads, value_heads = split_heads(qkv_rows)
    score_bias, bucket_picks = bias_of(table, row_count)
    same_doc = same_of(lengths, row_count)
    scores = scores_of(query_heads, key_heads, score_bias, same_doc)
    soft_rows = jnp.exp(scores - log_total)
    value_grad = jnp.einsum(
        "hts,thd->shd",
        soft_rows.astype(jnp.bfloat16),
        attended_grad,
        preferred_element_type=jnp.float32,
    )
    prob_grad = jnp.einsum(
        "thd,shd->hts", attended_grad, value_heads, preferred_element_type=jnp.float32
    )
    score_grad = (
        soft_rows * (prob_grad - jnp.sum(soft_rows * prob_grad, axis=-1, keepdims=True))
    ).astype(jnp.bfloat16)
    query_grad = jnp.einsum(
        "hts,shd->thd", score_grad, key_heads, preferred_element_type=jnp.float32
    ) * (1.0 / math.sqrt(HD))
    key_grad = jnp.einsum(
        "hts,thd->shd", score_grad, query_heads, preferred_element_type=jnp.float32
    ) * (1.0 / math.sqrt(HD))
    table_grad = jnp.einsum(
        "tsb,hts->bh", bucket_picks, score_grad, preferred_element_type=jnp.float32
    ).reshape(-1)
    qkv_grad = jnp.concatenate(
        [
            query_grad.reshape(row_count, model_width),
            key_grad.reshape(row_count, model_width),
            value_grad.reshape(row_count, model_width),
        ],
        axis=1,
    ).astype(jnp.bfloat16)
    normed_grad = jnp.einsum("te,de->td", qkv_grad, w_qkv, preferred_element_type=jnp.float32)
    gain_one_grad = jnp.sum(normed_grad * layer_in * scale_one, axis=0)
    input_grad = middle_grad + rms_back(
        normed_grad * gain_one.astype(jnp.float32), layer_in, scale_one
    )
    small_grads = (gain_one_grad, table_grad, gain_two_grad)
    factor_rows = (normed, qkv_grad, attended, branch_grad, routed, logit_grad)
    expert_rows = (arrived_rows, hidden_grad, active_low, rows_grad)
    return (input_grad, small_grads, factor_rows, expert_rows)


def shared_from(small_grads, factor_rows):
    normed, qkv_grad, attended, branch_grad, routed, logit_grad = factor_rows
    qkv_weight_grad = jnp.einsum("td,te->de", normed, qkv_grad, preferred_element_type=jnp.float32)
    out_weight_grad = jnp.einsum(
        "td,te->de", attended, branch_grad, preferred_element_type=jnp.float32
    )
    route_weight_grad = jnp.einsum(
        "td,te->de", routed, logit_grad, preferred_element_type=jnp.float32
    )
    return (
        small_grads[0],
        qkv_weight_grad,
        small_grads[1],
        out_weight_grad,
        small_grads[2],
        route_weight_grad,
    )


def stack_states(*states):
    return jnp.stack(states)


def join_rows(*parts):
    return jnp.concatenate(parts, axis=0)


def add_arrays(first_one, second_one):
    return first_one + second_one


def shards(
    tokens,
    out_grad,
    routes,
    doc_lengths,
    norm_attn,
    attn_qkv,
    rel_bias,
    attn_out,
    norm_ffn,
    router,
    expert_in,
    expert_out,
):
    section_index = lax.axis_index("section")
    micro_count = tokens.shape[0]
    owned = (norm_attn[0], attn_qkv[0], rel_bias[0], attn_out[0], norm_ffn[0], router[0])
    weights = (
        lax.all_gather(owned[0], "dp", axis=0, tiled=True),
        lax.all_gather(owned[1], "dp", axis=0, tiled=True),
        lax.all_gather(owned[2], "dp", axis=0, tiled=True),
        lax.all_gather(owned[3], "dp", axis=0, tiled=True),
        lax.all_gather(owned[4], "dp", axis=0, tiled=True),
        lax.all_gather(owned[5], "dp", axis=0, tiled=True),
    )
    weight_in = expert_in[0, 0]
    weight_back = expert_out[0, 0]
    route_table = routes[0, :, :, 0]
    length_table = doc_lengths[:, 0]
    received = jnp.zeros(tokens.shape[1:], jnp.bfloat16)
    outputs = jnp.zeros(tokens.shape, jnp.bfloat16)
    stored = []
    for moment in range(micro_count + 1):
        micro_index = jnp.clip(moment - section_index, 0, micro_count - 1)
        is_valid = (moment - section_index >= 0) & (moment - section_index < micro_count)
        fresh_rows = tokens[min(moment, micro_count - 1)]
        layer_in = jnp.where(section_index == 0, fresh_rows, received).astype(jnp.float32)
        route_now = lax.dynamic_index_in_dim(route_table, micro_index, 0, keepdims=False)
        lengths = lax.dynamic_index_in_dim(length_table, micro_index, 0, keepdims=False)
        result, kept_state = layer_forward(
            layer_in, weights, route_now, lengths, weight_in, weight_back
        )
        result_low = result.astype(jnp.bfloat16)
        current = lax.dynamic_index_in_dim(outputs, micro_index, 0, keepdims=False)
        outputs = lax.dynamic_update_index_in_dim(
            outputs, jnp.where(is_valid, result_low, current), micro_index, 0
        )
        stored.append(kept_state)
        if moment < micro_count:
            received = shifted(result_low, "section", 1)
    stacked = jax.tree.map(stack_states, *stored)
    back_weights = (
        lax.all_gather(owned[0], "dp", axis=0, tiled=True),
        lax.all_gather(owned[1], "dp", axis=0, tiled=True),
        lax.all_gather(owned[2], "dp", axis=0, tiled=True),
        lax.all_gather(owned[3], "dp", axis=0, tiled=True),
        lax.all_gather(owned[4], "dp", axis=0, tiled=True),
        lax.all_gather(owned[5], "dp", axis=0, tiled=True),
    )
    small_total = (
        jnp.zeros(owned[0].shape[:0] + (weights[0].shape[0],), jnp.float32),
        jnp.zeros(weights[2].shape, jnp.float32),
        jnp.zeros(weights[4].shape, jnp.float32),
    )
    factor_list = []
    expert_list = []
    input_store = jnp.zeros(tokens.shape, jnp.float32)
    received_grad = jnp.zeros(tokens.shape[1:], jnp.bfloat16)
    for moment in range(micro_count + 1):
        micro_raw = moment - 1 + section_index
        micro_index = jnp.clip(micro_raw, 0, micro_count - 1)
        is_valid = (micro_raw >= 0) & (micro_raw < micro_count)
        state_index = jnp.clip(moment - 1 + 2 * section_index, 0, micro_count)

        def pick_state(whole_stack):
            return lax.dynamic_index_in_dim(whole_stack, state_index, 0, keepdims=False)

        kept_state = jax.tree.map(pick_state, stacked)
        cotangent = lax.dynamic_index_in_dim(out_grad, micro_index, 0, keepdims=False).astype(
            jnp.float32
        )
        from_output = jnp.where(is_valid, cotangent, 0.0)
        upstream = jnp.where(section_index == 1, from_output, received_grad.astype(jnp.float32))
        route_now = lax.dynamic_index_in_dim(route_table, micro_index, 0, keepdims=False)
        lengths = lax.dynamic_index_in_dim(length_table, micro_index, 0, keepdims=False)
        input_grad, small_grads, factor_rows, expert_rows = layer_backward(
            upstream, kept_state, back_weights, route_now, lengths, weight_in, weight_back
        )
        small_total = jax.tree.map(add_arrays, small_total, small_grads)
        factor_list.append(factor_rows)
        expert_list.append(expert_rows)
        current = lax.dynamic_index_in_dim(input_store, micro_index, 0, keepdims=False)
        input_store = lax.dynamic_update_index_in_dim(
            input_store, jnp.where(is_valid, input_grad, current), micro_index, 0
        )
        if moment < micro_count:
            received_grad = shifted(input_grad.astype(jnp.bfloat16), "section", -1)
    arrived_all, hidden_grad_all, active_all, rows_grad_all = jax.tree.map(join_rows, *expert_list)
    in_total = jnp.einsum(
        "rd,rf->df", arrived_all, hidden_grad_all, preferred_element_type=jnp.float32
    )
    back_total = jnp.einsum(
        "rf,rd->fd", active_all, rows_grad_all, preferred_element_type=jnp.float32
    )
    joined = jax.tree.map(join_rows, *factor_list)
    grad_totals = shared_from(small_total, joined)
    summed = (
        lax.psum_scatter(grad_totals[0], "dp", scatter_dimension=0, tiled=True),
        lax.psum_scatter(grad_totals[1], "dp", scatter_dimension=0, tiled=True),
        lax.psum_scatter(grad_totals[2], "dp", scatter_dimension=0, tiled=True),
        lax.psum_scatter(grad_totals[3], "dp", scatter_dimension=0, tiled=True),
        lax.psum_scatter(grad_totals[4], "dp", scatter_dimension=0, tiled=True),
        lax.psum_scatter(grad_totals[5], "dp", scatter_dimension=0, tiled=True),
    )
    return (
        outputs[None],
        input_store[None],
        summed[0][None],
        summed[1][None],
        summed[2][None],
        summed[3][None],
        summed[4][None],
        summed[5][None],
        in_total[None, None],
        back_total[None, None],
    )


def solution(mesh):
    placed = (
        P(None, "dp", None),
        P(None, "dp", None),
        P("section", None, "dp", None),
        P(None, "dp", None),
        P("section", "dp"),
        P("section", "dp", None),
        P("section", "dp"),
        P("section", "dp", None),
        P("section", "dp"),
        P("section", "dp", None),
        P("section", "dp", None, None),
        P("section", "dp", None, None),
    )
    return jax.shard_map(
        shards,
        mesh=mesh,
        in_specs=placed,
        out_specs=(
            P("section", None, "dp", None),
            P("section", None, "dp", None),
            P("section", "dp"),
            P("section", "dp", None),
            P("section", "dp"),
            P("section", "dp", None),
            P("section", "dp"),
            P("section", "dp", None),
            P("section", "dp", None, None),
            P("section", "dp", None, None),
        ),
        check_vma=False,
    )
```

profile of v0, /device:TPU:13, one launch (start us, length us, event | category | flops | bytes accessed | tf_op | source)
XLA Modules:
  0.0 977.3 jit_solution(6554547486149026566)
XLA Ops:
  15.1 26.6 %all-reduce.7 = (bf16[768]{0:T(1024)(128)(2,1)S(1)}, bf16[384]{0:T(512)(128)(2,1)S(1)}, bf16[768]{0:T(1024)(128)(2,1)S(1)}) all-reduce(bf16[768]{0:T(1024)(128)(2,1)S(1)} %dynamic-update-slice, bf16[384]{0:T(512)(128)(2,1)S(1)} %dynamic-update-slice.1, bf16[768]{0:T(1024)(128)(2,1)S(1)} %dynamic-update-slice.2), channel_id=2, replica_groups=mesh['section'=2,'dp'=16] {'dp'}, use_global_device_ids=true, to_apply=%add | all-reduce | flops 1920 | bytes 7680
  45.5 37.2 %all-gather.9.cloned.1.call-done = bf16[1,768,2304]{2,1,0:T(8,128)(2,1)} async-done(((bf16[1,48,2304]{2,1,0:T(8,128)(2,1)}), bf16[1,768,2304]{2,1,0:T(8,128)(2,1)}) %all-gather.9.cloned.1.call-update) | async-done | bytes 3538960 | tf_op jit(solution)/shard_map/all_gather | solution.py:347
  87.4 51.7 %all-gather.11.cloned.1.call-done = bf16[1,768,768]{2,1,0:T(8,128)(2,1)} async-done(((bf16[1,48,768]{2,1,0:T(8,128)(2,1)}), bf16[1,768,768]{2,1,0:T(8,128)(2,1)}) %all-gather.11.cloned.1.call-update) | async-done | bytes 1179664 | tf_op jit(solution)/shard_map/all_gather | solution.py:349
  142.6 5.0 all-to-all-start
  148.3 34.6 %all-gather.5 = bf16[1,768,4]{2,0,1:T(2,128)(2,1)} all-gather(bf16[1,48,4]{2,0,1:T(2,128)(2,1)} %copy.342), channel_id=7, replica_groups=mesh['section'=2,'dp'=16] {'dp'}, dimensions={1}, use_global_device_ids=true | all-gather | bytes 6528 | tf_op jit(solution)/shard_map/all_gather | solution.py:351
  210.1 8.2 all-to-all-start.1
  220.4 7.5 all-to-all-done.1
  230.9 10.8 %collective-permute-done = bf16[64,768]{1,0:T(8,128)(2,1)S(1)} collective-permute-done((bf16[64,768]{1,0:T(8,128)(2,1)S(1)}, bf16[64,768]{1,0:T(8,128)(2,1)S(1)}, u32[]{:S(2)}, u32[]{:S(2)}) %collective-permute-start) | collective-permute-done | bytes 98336 | tf_op jit(solution)/shard_map/ppermute | solution.py:22
  251.5 4.8 all-to-all-start.2
  262.5 8.7 all-to-all-done.2
  275.1 4.8 all-to-all-start.3
  282.5 12.3 %all-to-all-done.3 = bf16[16,24,768]{2,1,0:T(8,128)(2,1)} async-done(((bf16[16,24,768]{2,1,0:T(8,128)(2,1)}), bf16[16,24,768]{2,1,0:T(8,128)(2,1)}, u32[]{:S(2)}, u32[]{:S(2)}) %all-to-all-start.3) | async-done | bytes 589856 | tf_op jit(solution)/shard_map/all_to_all | solution.py:154
  328.4 7.2 all-to-all-done.4
  337.5 4.8 all-to-all-start.6
  350.9 6.3 all-to-all-done.6
  362.3 4.9 all-to-all-start.7
  372.8 9.3 all-to-all-done.7
  382.1 5.1 all-to-all-start.5
  438.5 4.9 all-to-all-start.8
  446.2 12.4 %all-to-all-done.8 = bf16[16,24,768]{2,1,0:T(8,128)(2,1)} async-done(((bf16[16,24,768]{2,1,0:T(8,128)(2,1)}), bf16[16,24,768]{2,1,0:T(8,128)(2,1)}, u32[]{:S(2)}, u32[]{:S(2)}) %all-to-all-start.8) | async-done | bytes 589856 | tf_op jit(solution)/shard_map/all_to_all | solution.py:219
  516.0 4.6 collective-permute-start.3
  523.4 6.7 all-to-all-start.10
  536.0 9.0 all-to-all-done.10
  549.3 4.8 all-to-all-start.11
  560.7 8.4 all-to-all-done.11
  592.5 4.9 fusion.193
  603.7 78.9 %reduce-scatter.10.cloned.1.call-done = f32[48,4]{1,0:T(8,128)} async-done(((f32[768,4]{1,0:T(8,128)}), f32[48,4]{1,0:T(8,128)}) %reduce-scatter.10.cloned.1.call-update) | async-done | bytes 784
  684.0 5.2 fusion.48
  689.3 4.7 fusion.43
  698.2 52.1 %all-reduce.6 = (f32[768]{0:T(1024)S(1)}, f32[384]{0:T(512)S(1)}, f32[768]{0:T(1024)S(1)}) all-reduce(f32[768]{0:T(1024)S(1)} %add_add_fusion.1, f32[384]{0:T(512)S(1)} %add.515, f32[768]{0:T(1024)S(1)} %add_add_fusion), channel_id=8, replica_groups=mesh['section'=2,'dp'=16] {'dp'}, use_global_device_ids=true, to_apply=%region_67.68.clone | all-reduce | flops 1920 | bytes 15360
  752.1 63.3 %reduce-scatter.8.cloned.1.call-done = f32[48,768]{1,0:T(8,128)} async-done(((f32[768,768]{1,0:T(8,128)}), f32[48,768]{1,0:T(8,128)}) %reduce-scatter.8.cloned.1.call-update) | async-done | bytes 147472 | tf_op jit(solution)/shard_map/reduce_scatter | solution.py:438
  815.4 154.9 %reduce-scatter.6.cloned.1.call-done = f32[48,2304]{1,0:T(8,128)} async-done(((f32[768,2304]{1,0:T(8,128)}), f32[48,2304]{1,0:T(8,128)}) %reduce-scatter.6.cloned.1.call-update) | async-done | bytes 442384 | tf_op jit(solution)/shard_map/reduce_scatter | solution.py:436
  (679 shorter events, 293.6 us)
Async XLA Ops:
  7.2 201.2 %copy-start = (bf16[1,1,768,768]{3,2,1,0:T(8,128)(2,1)S(1)}, bf16[1,1,768,768]{3,2,1,0:T(8,128)(2,1)}, u32[]{:S(2)}) copy-start(bf16[1,1,768,768]{3,2,1,0:T(8,128)(2,1)} %param.24) | copy-start | bytes 3538948
  7.2 75.5 %all-gather.9.cloned.1.call-start = ((), (), s32[]{:S(2)}) async-start(), calls=%async_computation.17 | async-start | bytes 3760128 | tf_op jit(solution)/shard_map/all_gather | solution.py:347
  8.0 131.1 %all-gather.11.cloned.1.call-start = ((), (), s32[]{:S(2)}) async-start(), calls=%async_computation.18 | async-start | bytes 1253376 | tf_op jit(solution)/shard_map/all_gather | solution.py:349
  43.0 39.7 %copy-start.135 = (s32[64]{0:T(128)}, s32[64]{0:T(128)S(1)}, u32[]{:S(2)}) copy-start(s32[64]{0:T(128)S(1)} %get-tuple-element.120) | copy-start | bytes 772
  43.3 98.2 %copy-start.97 = (s32[4,24]{1,0:T(4,128)}, s32[4,24]{1,0:T(4,128)S(1)}, u32[]{:S(2)}) copy-start(s32[4,24]{1,0:T(4,128)S(1)} %multiply_add_fusion.4) | copy-start | bytes 1156
  45.4 96.1 %copy-start.166 = (s32[64]{0:T(128)}, s32[64]{0:T(128)S(1)}, u32[]{:S(2)}) copy-start(s32[64]{0:T(128)S(1)} %multiply_add_fusion.10) | copy-start | bytes 772
  87.0 53.8 %copy-start.107 = (f32[12,64]{1,0:T(8,128)}, f32[12,64]{1,0:T(8,128)S(1)}, u32[]{:S(2)}) copy-start(f32[12,64]{1,0:T(8,128)S(1)} %get-tuple-element.136) | copy-start | bytes 9220
  87.1 53.7 %copy-start.112 = (f32[12,64]{1,0:T(8,128)}, f32[12,64]{1,0:T(8,128)S(1)}, u32[]{:S(2)}) copy-start(f32[12,64]{1,0:T(8,128)S(1)} %fusion.235) | copy-start | bytes 9220
  87.4 55.2 %copy-start.75 = (bf16[12,64,64]{2,1,0:T(8,128)(2,1)}, bf16[12,64,64]{2,1,0:T(8,128)(2,1)S(1)}, u32[]{:S(2)}) copy-start(bf16[12,64,64]{2,1,0:T(8,128)(2,1)S(1)} %convolution_convert_fusion.11) | copy-start | bytes 294916
  140.8 87.2 %copy-start.17 = (f32[64,768]{1,0:T(8,128)}, f32[64,768]{1,0:T(8,128)S(1)}, u32[]{:S(2)}) copy-start(f32[64,768]{1,0:T(8,128)S(1)} %get-tuple-element.139) | copy-start | bytes 589828
  142.6 64.9 %copy-start.2 = (bf16[1,1,768,768]{3,2,1,0:T(8,128)(2,1)S(1)}, bf16[1,1,768,768]{3,2,1,0:T(8,128)(2,1)}, u32[]{:S(2)}) copy-start(bf16[1,1,768,768]{3,2,1,0:T(8,128)(2,1)} %param.23) | copy-start | bytes 3538948
  142.6 64.9 %all-to-all-start = ((bf16[16,24,768]{2,1,0:T(8,128)(2,1)}), bf16[16,24,768]{2,1,0:T(8,128)(2,1)S(1)}, u32[]{:S(2)}, u32[]{:S(2)}) async-start(bf16[16,24,768]{2,1,0:T(8,128)(2,1)} %bitcast.710), calls=%async_computation | async-start | bytes 1179648 | tf_op jit(solution)/shard_map/all_to_all | solution.py:145
  210.1 17.8 %all-to-all-start.1 = ((bf16[16,24,768]{2,1,0:T(8,128)(2,1)}), bf16[16,24,768]{2,1,0:T(8,128)(2,1)S(1)}, u32[]{:S(2)}, u32[]{:S(2)}) async-start(bf16[16,24,768]{2,1,0:T(8,128)(2,1)} %bitcast.21), calls=%async_computation.1 | async-start | bytes 1179648 | tf_op jit(solution)/shard_map/all_to_all | solution.py:154
  229.0 12.7 %collective-permute-start = (bf16[64,768]{1,0:T(8,128)(2,1)S(1)}, bf16[64,768]{1,0:T(8,128)(2,1)S(1)}, u32[]{:S(2)}, u32[]{:S(2)}) collective-permute-start(bf16[64,768]{1,0:T(8,128)(2,1)S(1)} %get-tuple-element.49), channel_id=1, source_target_pairs={{0,16},{1,17},{2,18},{3,19},{4,20},{5,21},{6,22},{7,23},{8,24},{9,... | collective-permute-start | bytes 294920 | tf_op jit(solution)/shard_map/ppermute | solution.py:22
  251.5 19.7 %all-to-all-start.2 = ((bf16[16,24,768]{2,1,0:T(8,128)(2,1)}), bf16[16,24,768]{2,1,0:T(8,128)(2,1)S(1)}, u32[]{:S(2)}, u32[]{:S(2)}) async-start(bf16[16,24,768]{2,1,0:T(8,128)(2,1)} %bitcast.713), calls=%async_computation.2 | async-start | bytes 1179648 | tf_op jit(solution)/shard_map/all_to_all | solution.py:145
  275.1 19.7 %all-to-all-start.3 = ((bf16[16,24,768]{2,1,0:T(8,128)(2,1)}), bf16[16,24,768]{2,1,0:T(8,128)(2,1)}, u32[]{:S(2)}, u32[]{:S(2)}) async-start(bf16[16,24,768]{2,1,0:T(8,128)(2,1)} %bitcast.750), calls=%async_computation.3 | async-start | bytes 1179648 | tf_op jit(solution)/shard_map/all_to_all | solution.py:154
  297.8 3.8 collective-permute-start.1
  316.2 19.4 %all-to-all-start.4 = ((bf16[16,24,768]{2,1,0:T(8,128)(2,1)}), bf16[16,24,768]{2,1,0:T(8,128)(2,1)S(1)}, u32[]{:S(2)}, u32[]{:S(2)}) async-start(bf16[16,24,768]{2,1,0:T(8,128)(2,1)} %bitcast.711), calls=%async_computation.4 | async-start | bytes 1179648 | tf_op jit(solution)/shard_map/all_to_all | solution.py:145
  337.5 19.7 %all-to-all-start.6 = ((bf16[16,24,768]{2,1,0:T(8,128)(2,1)}), bf16[16,24,768]{2,1,0:T(8,128)(2,1)}, u32[]{:S(2)}, u32[]{:S(2)}) async-start(bf16[16,24,768]{2,1,0:T(8,128)(2,1)} %bitcast.712), calls=%async_computation.6 | async-start | bytes 1179648 | tf_op jit(solution)/shard_map/all_to_all | solution.py:219
  362.3 19.8 %all-to-all-start.7 = ((bf16[16,24,768]{2,1,0:T(8,128)(2,1)}), bf16[16,24,768]{2,1,0:T(8,128)(2,1)}, u32[]{:S(2)}, u32[]{:S(2)}) async-start(bf16[16,24,768]{2,1,0:T(8,128)(2,1)} %bitcast.81), calls=%async_computation.7 | async-start | bytes 1179648 | tf_op jit(solution)/shard_map/all_to_all | solution.py:232
  382.1 19.9 %all-to-all-start.5 = ((bf16[16,24,768]{2,1,0:T(8,128)(2,1)}), bf16[16,24,768]{2,1,0:T(8,128)(2,1)}, u32[]{:S(2)}, u32[]{:S(2)}) async-start(bf16[16,24,768]{2,1,0:T(8,128)(2,1)} %bitcast.747), calls=%async_computation.5 | async-start | bytes 1179648 | tf_op jit(solution)/shard_map/all_to_all | solution.py:154
  431.4 4.9 collective-permute-start.2
  438.5 20.1 %all-to-all-start.8 = ((bf16[16,24,768]{2,1,0:T(8,128)(2,1)}), bf16[16,24,768]{2,1,0:T(8,128)(2,1)}, u32[]{:S(2)}, u32[]{:S(2)}) async-start(bf16[16,24,768]{2,1,0:T(8,128)(2,1)} %bitcast.715), calls=%async_computation.8 | async-start | bytes 1179648 | tf_op jit(solution)/shard_map/all_to_all | solution.py:219
  462.9 25.1 %all-to-all-start.9 = ((bf16[16,24,768]{2,1,0:T(8,128)(2,1)}), bf16[16,24,768]{2,1,0:T(8,128)(2,1)}, u32[]{:S(2)}, u32[]{:S(2)}) async-start(bf16[16,24,768]{2,1,0:T(8,128)(2,1)} %bitcast.749), calls=%async_computation.9 | async-start | bytes 1179648 | tf_op jit(solution)/shard_map/all_to_all | solution.py:232
  516.0 5.2 collective-permute-start.3
  523.4 21.6 %all-to-all-start.10 = ((bf16[16,24,768]{2,1,0:T(8,128)(2,1)}), bf16[16,24,768]{2,1,0:T(8,128)(2,1)}, u32[]{:S(2)}, u32[]{:S(2)}) async-start(bf16[16,24,768]{2,1,0:T(8,128)(2,1)} %bitcast.714), calls=%async_computation.10 | async-start | bytes 1179648 | tf_op jit(solution)/shard_map/all_to_all | solution.py:219
  549.3 19.7 %all-to-all-start.11 = ((bf16[16,24,768]{2,1,0:T(8,128)(2,1)}), bf16[16,24,768]{2,1,0:T(8,128)(2,1)}, u32[]{:S(2)}, u32[]{:S(2)}) async-start(bf16[16,24,768]{2,1,0:T(8,128)(2,1)} %bitcast.748), calls=%async_computation.11 | async-start | bytes 1179648 | tf_op jit(solution)/shard_map/all_to_all | solution.py:232
  554.1 128.5 %reduce-scatter.10.cloned.1.call-start = ((), (), s32[]{:S(2)}) async-start(), calls=%async_computation.19 | async-start | bytes 417792
  560.6 254.8 %reduce-scatter.8.cloned.1.call-start = ((), (), s32[]{:S(2)}) async-start(), calls=%async_computation.16 | async-start | bytes 2506752 | tf_op jit(solution)/shard_map/reduce_scatter | solution.py:438
  577.2 393.1 %reduce-scatter.6.cloned.1.call-start = ((), (), s32[]{:S(2)}) async-start(), calls=%async_computation.15 | async-start | bytes 7520256 | tf_op jit(solution)/shard_map/reduce_scatter | solution.py:436
  694.6 57.4 %copy-start.74 = (f32[64,768]{1,0:T(8,128)S(1)}, f32[64,768]{1,0:T(8,128)}, u32[]{:S(2)}) copy-start(f32[64,768]{1,0:T(8,128)} %get-tuple-element.29) | copy-start | bytes 589828
  752.1 218.2 %copy-start.85 = (f32[1,2,64,768]{3,2,1,0:T(8,128)}, f32[1,2,64,768]{3,2,1,0:T(8,128)S(1)}, u32[]{:S(2)}) copy-start(f32[1,2,64,768]{3,2,1,0:T(8,128)S(1)} %bitcast_dynamic-update-slice_fusion) | copy-start | bytes 1179652
  (173 other events, 936.1 us)
Sparse Core Ops, SparseCore 0:
  10.9 71.8 all-gather.8
  85.5 53.5 all-gather.10
  560.7 121.8 reduce-scatter.9
  688.7 126.6 reduce-scatter.7
  821.2 149.0 reduce-scatter.5
where the time goes:
time: 994 us; the launch traced here: 977 us
  waiting for transfers between devices  483 us (49%)
  blocking collectives  113 us (11%)
  matrix products  102 us (10%)
  local copies, waits for them, and re-layouts  98.1 us (10%)
  other arithmetic  87.1 us (9%)
  starting transfers between devices  74.7 us (8%)
  between operations  19.2 us (2%)
    reduce_scatter x1, waiting for transfers between devices, shards(): lax.psum_scatter(grad_totals[1], 'dp', scatter_dimension=0, tiled=True)  155 us
    unnamed x6, waiting for transfers between devices  80.3 us
    unnamed x2, blocking collectives  78.7 us
    reduce_scatter x1, waiting for transfers between devices, shards(): lax.psum_scatter(grad_totals[3], 'dp', scatter_dimension=0, tiled=True)  63.3 us
    all_gather x1, waiting for transfers between devices, shards(): lax.all_gather(owned[3], 'dp', axis=0, tiled=True)  51.7 us
    all_gather x1, waiting for transfers between devices, shards(): lax.all_gather(owned[1], 'dp', axis=0, tiled=True)  37.2 us
    all_gather x1, blocking collectives, shards(): lax.all_gather(owned[5], 'dp', axis=0, tiled=True)  34.6 us
    all_to_all x3, waiting for transfers between devices, layer_backward(): lax.all_to_all(outgoing, 'dp', split_axis=0, concat_axis=0, tiled=True)  27.6 us
  transfers between devices with their start and end apart: 21, of which 17 were waited for; matrix products, arithmetic and copies ran while one was open for 17% of the time, Pallas kernels for 0%

commit v1 on v0

--- a/solution.py
+++ b/solution.py
@@ -14,12 +14,6 @@
 
 EPSILON = 1e-06
 far_limits = np.array([8, 12, 16, 23, 32, 46, 64, 91], dtype=np.int32)
-
-
-def shifted(block, axis, distance):
-    devices = range(lax.axis_size(axis))
-    route = [(i - distance, i) for i in devices if i - distance in devices]
-    return lax.ppermute(block, axis, route)
 
 
 def buckets_of(row_count):
@@ -45,10 +39,14 @@
     return documents[:, None] == documents[None, :]
 
 
+def picks_of(row_count):
+    return (
+        buckets_of(row_count)[:, :, None] == jnp.arange(BUCKETS, dtype=jnp.int32)[None, None, :]
+    ).astype(jnp.bfloat16)
+
+
 def bias_of(table, row_count):
-    bucket_picks = (
-        buckets_of(row_count)[:, :, None] == jnp.arange(BUCKETS, dtype=jnp.int32)[None, None, :]
-    ).astype(jnp.bfloat16)
+    bucket_picks = picks_of(row_count)
     score_bias = jnp.einsum(
         "tsb,bh->hts",
         bucket_picks,
@@ -78,10 +76,9 @@
 
 def placement_of(route_now, expert_count, slot_count):
     row_count = route_now.shape[0]
-    picked = (route_now[:, None] == jnp.arange(expert_count, dtype=jnp.int32)[None, :]).astype(
-        jnp.int32
-    )
-    ranks = jnp.sum((jnp.cumsum(picked, axis=0) - 1) * picked, axis=1)
+    places = jnp.arange(row_count, dtype=jnp.int32)
+    earlier = (route_now[:, None] == route_now[None, :]) & (places[None, :] < places[:, None])
+    ranks = jnp.sum(earlier.astype(jnp.int32), axis=1)
     target = route_now * slot_count + ranks
     flat = (
         jnp.arange(expert_count * slot_count, dtype=jnp.int32)[:, None] == target[None, :]
@@ -127,8 +124,8 @@
     row_max = jnp.max(scores, axis=-1, keepdims=True)
     exp_rows = jnp.exp(scores - row_max)
     exp_total = jnp.sum(exp_rows, axis=-1, keepdims=True)
-    log_total = row_max + jnp.log(exp_total)
-    soft_low = (exp_rows / exp_total).astype(jnp.bfloat16)
+    soft_rows = exp_rows / exp_total
+    soft_low = soft_rows.astype(jnp.bfloat16)
     attended = jnp.einsum("hts,shd->thd", soft_low, value_heads, preferred_element_type=jnp.float32)
     attended = attended.reshape(row_count, model_width).astype(jnp.bfloat16)
     middle = layer_in + jnp.dot(attended, w_out, preferred_element_type=jnp.float32)
@@ -169,7 +166,7 @@
         scale_one,
         normed,
         qkv_rows,
-        log_total,
+        soft_rows,
         attended,
         middle,
         scale_two,
@@ -189,7 +186,7 @@
         scale_one,
         normed,
         qkv_rows,
-        log_total,
+        soft_rows,
         attended,
         middle,
         scale_two,
@@ -250,10 +247,7 @@
     ).astype(jnp.bfloat16)
     attended_grad = attended_grad.reshape(row_count, HEADS, HD)
     query_heads, key_heads, value_heads = split_heads(qkv_rows)
-    score_bias, bucket_picks = bias_of(table, row_count)
-    same_doc = same_of(lengths, row_count)
-    scores = scores_of(query_heads, key_heads, score_bias, same_doc)
-    soft_rows = jnp.exp(scores - log_total)
+    bucket_picks = picks_of(row_count)
     value_grad = jnp.einsum(
         "hts,thd->shd",
         soft_rows.astype(jnp.bfloat16),
@@ -313,16 +307,56 @@
     )
 
 
-def stack_states(*states):
-    return jnp.stack(states)
-
-
-def join_rows(*parts):
-    return jnp.concatenate(parts, axis=0)
-
-
-def add_arrays(first_one, second_one):
-    return first_one + second_one
+SMALL = 256
+
+
+def swap_cores(block):
+    return lax.ppermute(block, "section", [(0, 1), (1, 0)])
+
+
+def per_core(section_index, first_one, second_one):
+    return jnp.where(section_index == 0, first_one, second_one)
+
+
+def pack_columns(wide, square, columns):
+    small = jnp.concatenate(columns, axis=1)
+    small = jnp.pad(small, ((0, 0), (0, SMALL - small.shape[1])))
+    return jnp.concatenate([wide, square, small], axis=1)
+
+
+def spaced(table, group_count):
+    table = table.reshape(group_count, -1)
+    row_share = 2 * table.shape[1]
+    return jnp.pad(table, ((0, 0), (0, row_share - table.shape[1]))).reshape(-1, 1)
+
+
+def gather_rows(shard):
+    dp_count = lax.axis_size("dp")
+    copies = jnp.broadcast_to(shard[None], (dp_count,) + shard.shape)
+    got = lax.all_to_all(copies, "dp", split_axis=0, concat_axis=0, tiled=True)
+    return got.reshape(dp_count * shard.shape[0], shard.shape[1])
+
+
+def sum_rows(whole):
+    dp_count = lax.axis_size("dp")
+    parts = whole.reshape(dp_count, whole.shape[0] // dp_count, whole.shape[1])
+    got = lax.all_to_all(parts, "dp", split_axis=0, concat_axis=0, tiled=True)
+    return jnp.sum(got.astype(jnp.float32), axis=0)
+
+
+def unpack_weights(packed, width, expert_count):
+    dp_count = lax.axis_size("dp")
+    small = packed[:, 4 * width :]
+    table = small[:, 2].reshape(dp_count, -1)
+    table = table[:, : table.shape[1] // 2].reshape(-1)
+    return (
+        small[:, 0],
+        packed[:, : 3 * width],
+        table,
+        packed[:, 3 * width : 4 * width],
+        small[:, 1],
+        small[:, 3 : 3 + expert_count],
+    )
 
 
 def shards(
@@ -339,115 +373,115 @@
     expert_in,
     expert_out,
 ):
-    section_index = lax.axis_index("section")
-    micro_count = tokens.shape[0]
-    owned = (norm_attn[0], attn_qkv[0], rel_bias[0], attn_out[0], norm_ffn[0], router[0])
-    weights = (
-        lax.all_gather(owned[0], "dp", axis=0, tiled=True),
-        lax.all_gather(owned[1], "dp", axis=0, tiled=True),
-        lax.all_gather(owned[2], "dp", axis=0, tiled=True),
-        lax.all_gather(owned[3], "dp", axis=0, tiled=True),
-        lax.all_gather(owned[4], "dp", axis=0, tiled=True),
-        lax.all_gather(owned[5], "dp", axis=0, tiled=True),
-    )
-    weight_in = expert_in[0, 0]
-    weight_back = expert_out[0, 0]
+    core = lax.axis_index("section")
+    dp_count = lax.axis_size("dp")
+    width = tokens.shape[2]
+    expert_count = router.shape[2]
+    own_pack = pack_columns(
+        attn_qkv[0],
+        attn_out[0],
+        [norm_attn[0][:, None], norm_ffn[0][:, None], spaced(rel_bias[0], 1), router[0]],
+    )
+    half = own_pack.shape[1] // 2
+    first_half, second_half = own_pack[:, :half], own_pack[:, half:]
+    other_part = swap_cores(per_core(core, second_half, first_half))
+    part_zero = per_core(core, first_half, other_part)
+    part_one = per_core(core, other_part, second_half)
+
+    def whole_of(part):
+        mine = gather_rows(part)
+        theirs = swap_cores(mine)
+        packed = jnp.concatenate(
+            [per_core(core, mine, theirs), per_core(core, theirs, mine)], axis=1
+        )
+        return unpack_weights(packed, width, expert_count)
+
+    weights = [whole_of(part_zero), None]
+    other_in = swap_cores(expert_in[0, 0])
+    other_out = swap_cores(expert_out[0, 0])
+    ins = [per_core(core, expert_in[0, 0], other_in), per_core(core, other_in, expert_in[0, 0])]
+    outs = [
+        per_core(core, expert_out[0, 0], other_out),
+        per_core(core, other_out, expert_out[0, 0]),
+    ]
     route_table = routes[0, :, :, 0]
-    length_table = doc_lengths[:, 0]
-    received = jnp.zeros(tokens.shape[1:], jnp.bfloat16)
-    outputs = jnp.zeros(tokens.shape, jnp.bfloat16)
-    stored = []
-    for moment in range(micro_count + 1):
-        micro_index = jnp.clip(moment - section_index, 0, micro_count - 1)
-        is_valid = (moment - section_index >= 0) & (moment - section_index < micro_count)
-        fresh_rows = tokens[min(moment, micro_count - 1)]
-        layer_in = jnp.where(section_index == 0, fresh_rows, received).astype(jnp.float32)
-        route_now = lax.dynamic_index_in_dim(route_table, micro_index, 0, keepdims=False)
-        lengths = lax.dynamic_index_in_dim(length_table, micro_index, 0, keepdims=False)
-        result, kept_state = layer_forward(
-            layer_in, weights, route_now, lengths, weight_in, weight_back
+    other_route = swap_cores(per_core(core, route_table[1], route_table[0]))
+    own_route = per_core(core, route_table[0], route_table[1])
+    route_rows = [
+        per_core(core, own_route, other_route),
+        per_core(core, other_route, own_route),
+    ]
+    lengths = per_core(core, doc_lengths[0, 0], doc_lengths[1, 0])
+    layer_in = per_core(core, tokens[0], tokens[1]).astype(jnp.float32)
+    weights[1] = whole_of(part_one)
+    kept, lows = [], []
+    for layer in range(2):
+        result, state = layer_forward(
+            layer_in, weights[layer], route_rows[layer], lengths, ins[layer], outs[layer]
         )
-        result_low = result.astype(jnp.bfloat16)
-        current = lax.dynamic_index_in_dim(outputs, micro_index, 0, keepdims=False)
-        outputs = lax.dynamic_update_index_in_dim(
-            outputs, jnp.where(is_valid, result_low, current), micro_index, 0
+        low = result.astype(jnp.bfloat16)
+        lows.append(low)
+        kept.append(state)
+        layer_in = low.astype(jnp.float32)
+
+    def sorted_out(pair):
+        mine = per_core(core, pair[0], pair[1])
+        theirs = swap_cores(per_core(core, pair[1], pair[0]))
+        return jnp.stack([per_core(core, mine, theirs), per_core(core, theirs, mine)])
+
+    upstream = per_core(core, out_grad[0], out_grad[1]).astype(jnp.float32)
+    input_grads, expert_rows, summed = [None, None], [None, None], [None, None]
+    for layer in (1, 0):
+        input_grad, small_grads, factor_rows, expert_rows[layer] = layer_backward(
+            upstream,
+            kept[layer],
+            weights[layer],
+            route_rows[layer],
+            lengths,
+            ins[layer],
+            outs[layer],
         )
-        stored.append(kept_state)
-        if moment < micro_count:
-            received = shifted(result_low, "section", 1)
-    stacked = jax.tree.map(stack_states, *stored)
-    back_weights = (
-        lax.all_gather(owned[0], "dp", axis=0, tiled=True),
-        lax.all_gather(owned[1], "dp", axis=0, tiled=True),
-        lax.all_gather(owned[2], "dp", axis=0, tiled=True),
-        lax.all_gather(owned[3], "dp", axis=0, tiled=True),
-        lax.all_gather(owned[4], "dp", axis=0, tiled=True),
-        lax.all_gather(owned[5], "dp", axis=0, tiled=True),
-    )
-    small_total = (
-        jnp.zeros(owned[0].shape[:0] + (weights[0].shape[0],), jnp.float32),
-        jnp.zeros(weights[2].shape, jnp.float32),
-        jnp.zeros(weights[4].shape, jnp.float32),
-    )
-    factor_list = []
-    expert_list = []
-    input_store = jnp.zeros(tokens.shape, jnp.float32)
-    received_grad = jnp.zeros(tokens.shape[1:], jnp.bfloat16)
-    for moment in range(micro_count + 1):
-        micro_raw = moment - 1 + section_index
-        micro_index = jnp.clip(micro_raw, 0, micro_count - 1)
-        is_valid = (micro_raw >= 0) & (micro_raw < micro_count)
-        state_index = jnp.clip(moment - 1 + 2 * section_index, 0, micro_count)
-
-        def pick_state(whole_stack):
-            return lax.dynamic_index_in_dim(whole_stack, state_index, 0, keepdims=False)
-
-        kept_state = jax.tree.map(pick_state, stacked)
-        cotangent = lax.dynamic_index_in_dim(out_grad, micro_index, 0, keepdims=False).astype(
-            jnp.float32
-        )
-        from_output = jnp.where(is_valid, cotangent, 0.0)
-        upstream = jnp.where(section_index == 1, from_output, received_grad.astype(jnp.float32))
-        route_now = lax.dynamic_index_in_dim(route_table, micro_index, 0, keepdims=False)
-        lengths = lax.dynamic_index_in_dim(length_table, micro_index, 0, keepdims=False)
-        input_grad, small_grads, factor_rows, expert_rows = layer_backward(
-            upstream, kept_state, back_weights, route_now, lengths, weight_in, weight_back
-        )
-        small_total = jax.tree.map(add_arrays, small_total, small_grads)
-        factor_list.append(factor_rows)
-        expert_list.append(expert_rows)
-        current = lax.dynamic_index_in_dim(input_store, micro_index, 0, keepdims=False)
-        input_store = lax.dynamic_update_index_in_dim(
-            input_store, jnp.where(is_valid, input_grad, current), micro_index, 0
-        )
-        if moment < micro_count:
-            received_grad = shifted(input_grad.astype(jnp.bfloat16), "section", -1)
-    arrived_all, hidden_grad_all, active_all, rows_grad_all = jax.tree.map(join_rows, *expert_list)
+        input_grads[layer] = input_grad
+        upstream = input_grad.astype(jnp.bfloat16).astype(jnp.float32)
+        totals = shared_from(small_grads, factor_rows)
+        packed = pack_columns(
+            totals[1],
+            totals[3],
+            [totals[0][:, None], totals[4][:, None], spaced(totals[2], dp_count), totals[5]],
+        ).astype(jnp.bfloat16)
+        left, right = packed[:, :half], packed[:, half:]
+        theirs = swap_cores(per_core(core, right, left))
+        mine = per_core(core, left, right)
+        both = (mine.astype(jnp.float32) + theirs.astype(jnp.float32)).astype(jnp.bfloat16)
+        summed[layer] = sum_rows(both)
+
+    def joined_rows(index):
+        mine = per_core(core, expert_rows[0][index], expert_rows[1][index])
+        theirs = swap_cores(per_core(core, expert_rows[1][index], expert_rows[0][index]))
+        return jnp.concatenate([mine, theirs], axis=0)
+
+    arrived_all, hidden_grad_all, active_all, rows_grad_all = [joined_rows(i) for i in range(4)]
     in_total = jnp.einsum(
         "rd,rf->df", arrived_all, hidden_grad_all, preferred_element_type=jnp.float32
     )
     back_total = jnp.einsum(
         "rf,rd->fd", active_all, rows_grad_all, preferred_element_type=jnp.float32
     )
-    joined = jax.tree.map(join_rows, *factor_list)
-    grad_totals = shared_from(small_total, joined)
-    summed = (
-        lax.psum_scatter(grad_totals[0], "dp", scatter_dimension=0, tiled=True),
-        lax.psum_scatter(grad_totals[1], "dp", scatter_dimension=0, tiled=True),
-        lax.psum_scatter(grad_totals[2], "dp", scatter_dimension=0, tiled=True),
-        lax.psum_scatter(grad_totals[3], "dp", scatter_dimension=0, tiled=True),
-        lax.psum_scatter(grad_totals[4], "dp", scatter_dimension=0, tiled=True),
-        lax.psum_scatter(grad_totals[5], "dp", scatter_dimension=0, tiled=True),
-    )
+    outputs = sorted_out(lows)
+    input_store = sorted_out(input_grads)
+    mine = per_core(core, summed[0], summed[1])
+    theirs = swap_cores(per_core(core, summed[1], summed[0]))
+    total = jnp.concatenate([per_core(core, mine, theirs), per_core(core, theirs, mine)], axis=1)
+    small = total[:, 4 * width :]
     return (
         outputs[None],
         input_store[None],
-        summed[0][None],
-        summed[1][None],
-        summed[2][None],
-        summed[3][None],
-        summed[4][None],
-        summed[5][None],
+        small[None, :, 0],
+        total[None, :, : 3 * width],
+        small[None, : rel_bias.shape[1], 2],
+        total[None, :, 3 * width : 4 * width],
+        small[None, :, 1],
+        small[None, :, 3 : 3 + expert_count],
         in_total[None, None],
         back_total[None, None],
     )

time: 994 us -> 536 us (0.54)
  waiting for transfers between devices: 483 us -> 192 us
  local copies, waits for them, and re-layouts: 98.1 us -> 40.9 us
  other arithmetic: 87.1 us -> 43 us
  matrix products: 102 us -> 73.9 us
  starting transfers between devices: 74.7 us -> 54.8 us
  between operations: 19.2 us -> 2.61 us
    reduce_scatter x2 -> x0, waiting for transfers between devices: 218 us -> none  [the longest x1 155 us: shards(): lax.psum_scatter(grad_totals[1], 'dp', scatter_dimension=0, tiled=True)]
    all_to_all x0 -> x3, waiting for transfers between devices: none -> 137 us  [the longest x2 87.6 us: sum_rows(): got = lax.all_to_all(parts, 'dp', split_axis=0, concat_axis=0, tiled=True)]
    all_to_all x0 -> x4, blocking collectives: none -> 120 us  [the longest x1 63.4 us: gather_rows(): got = lax.all_to_all(copies, 'dp', split_axis=0, concat_axis=0, tiled=True)]
    all_gather x2 -> x0, waiting for transfers between devices: 88.9 us -> none  [the longest x1 51.7 us: shards(): lax.all_gather(owned[3], 'dp', axis=0, tiled=True)]
    unnamed x6 -> x0, waiting for transfers between devices: 80.3 us -> none
    unnamed x2 -> x0, blocking collectives: 78.7 us -> none
    all_gather x1 -> x0, blocking collectives: 34.6 us -> none  [shards(): lax.all_gather(owned[5], 'dp', axis=0, tiled=True)]
    another operation x32 -> x3, other arithmetic: 32 us -> 0.23 us  [the longest x20 19 us: stack_states(): return jnp.stack(states)]
  transfers between devices with their start and end apart: 21 -> 23, of which waited for: 17 -> 14; matrix products, arithmetic and copies ran while one was open for 17% -> 18% of each run, Pallas kernels for 0% -> 0%
where the time goes in v1:
time: 536 us; the launch traced here: 527 us
  waiting for transfers between devices  192 us (36%)
  blocking collectives  120 us (22%)
  matrix products  73.9 us (14%)
  starting transfers between devices  54.8 us (10%)
  other arithmetic  43 us (8%)
  local copies, waits for them, and re-layouts  40.9 us (8%)
    all_to_all x2, waiting for transfers between devices, sum_rows(): got = lax.all_to_all(parts, 'dp', split_axis=0, concat_axis=0, tiled=True)  87.6 us
    all_to_all x1, blocking collectives, gather_rows(): got = lax.all_to_all(copies, 'dp', split_axis=0, concat_axis=0, tiled=True)  63.4 us
    all_to_all x1, waiting for transfers between devices, gather_rows(): got = lax.all_to_all(copies, 'dp', split_axis=0, concat_axis=0, tiled=True)  49.7 us
    all_to_all x1, blocking collectives, layer_backward(): lax.all_to_all(outgoing, 'dp', split_axis=0, concat_axis=0, tiled=True)  20.4 us
    all_to_all x1, blocking collectives, layer_forward(): lax.all_to_all(outgoing, 'dp', split_axis=0, concat_axis=0, tiled=True)  19.6 us
    select_n x14, other arithmetic, per_core(): return jnp.where(section_index == 0, first_one, second_one)  17.1 us
    all_to_all x1, blocking collectives, layer_backward(): lax.all_to_all(copy_grad.reshape(dp_count, slot_count, model_width), 'dp'...  16.9 us
    ppermute x15, starting transfers between devices, swap_cores(): return lax.ppermute(block, 'section', [(0, 1), (1, 0)])  14.3 us
  transfers between devices with their start and end apart: 23, of which 14 were waited for; matrix products, arithmetic and copies ran while one was open for 18% of the time, Pallas kernels for 0%

profile of v1, /device:TPU:13, one launch (start us, length us, event | category | flops | bytes accessed | tf_op | source)
XLA Modules:
  0.0 527.2 jit_solution(1713499043921298417)
XLA Ops:
  6.2 63.4 %all_to_all.60 = bf16[16,48,1664]{2,1,0:T(8,128)(2,1)S(1)} all-to-all(bf16[16,48,1664]{2,1,0:T(8,128)(2,1)S(1)} %broadcast_in_dim.66), channel_id=1, replica_groups=mesh['section'=2,'dp'=16] {'dp'}, dimensions={0} | all-to-all | bytes 5111808 | tf_op jit(solution)/shard_map/all_to_all | solution.py:336
  71.4 5.0 all-to-all-start.3
  76.3 2.6 collective-permute-start.1
  84.4 49.7 %all-to-all-done.3 = bf16[16,48,1664]{2,1,0:T(8,128)(2,1)} async-done(((bf16[16,48,1664]{2,1,0:T(8,128)(2,1)}), bf16[16,48,1664]{2,1,0:T(8,128)(2,1)}, u32[]{:S(2)}, u32[]{:S(2)}) %all-to-all-start.3) | async-done | bytes 2555936 | tf_op jit(solution)/shard_map/all_to_all | solution.py:336
  135.6 4.4 broadcast_select_fusion.4
  152.6 4.3 all-to-all-start.1
  158.7 13.4 %all-to-all-done.1 = bf16[16,24,768]{2,1,0:T(8,128)(2,1)S(1)} async-done(((bf16[16,24,768]{2,1,0:T(8,128)(2,1)}), bf16[16,24,768]{2,1,0:T(8,128)(2,1)S(1)}, u32[]{:S(2)}, u32[]{:S(2)}) %all-to-all-start.1) | async-done | bytes 589856 | tf_op jit(solution)/shard_map/all_to_all | solution.py:142
  172.1 2.5 fusion.58
  174.7 3.4 convolution_convert_fusion.9
  178.1 4.9 all-to-all-start.2
  183.0 4.5 broadcast_select_fusion.2
  195.3 3.9 all-to-all-done.2
  201.5 2.8 convolution_convert_fusion.2
  210.1 19.6 %all_to_all.61 = bf16[16,24,768]{2,1,0:T(8,128)(2,1)S(1)} all-to-all(bf16[16,24,768]{2,1,0:T(8,128)(2,1)S(1)} %bitcast.254), channel_id=1, replica_groups=mesh['section'=2,'dp'=16] {'dp'}, dimensions={0} | all-to-all | bytes 1179648 | tf_op jit(solution)/shard_map/all_to_all | solution.py:142
  233.7 5.1 all-to-all-start.5
  240.8 9.9 %all-to-all-done.5 = bf16[16,24,768]{2,1,0:T(8,128)(2,1)S(1)} async-done(((bf16[16,24,768]{2,1,0:T(8,128)(2,1)}), bf16[16,24,768]{2,1,0:T(8,128)(2,1)S(1)}, u32[]{:S(2)}, u32[]{:S(2)}) %all-to-all-start.5) | async-done | bytes 589856 | tf_op jit(solution)/shard_map/all_to_all | solution.py:151
  253.7 20.4 %all_to_all.62 = bf16[16,24,768]{2,1,0:T(8,128)(2,1)S(1)} all-to-all(bf16[16,24,768]{2,1,0:T(8,128)(2,1)S(1)} %bitcast.255), channel_id=1, replica_groups=mesh['section'=2,'dp'=16] {'dp'}, dimensions={0} | all-to-all | bytes 1179648 | tf_op jit(solution)/shard_map/all_to_all | solution.py:216
  276.4 16.9 %all_to_all.63 = bf16[16,24,768]{2,1,0:T(8,128)(2,1)S(1)} all-to-all(bf16[16,24,768]{2,1,0:T(8,128)(2,1)S(1)} %bitcast.271), channel_id=1, replica_groups=mesh['section'=2,'dp'=16] {'dp'}, dimensions={0} | all-to-all | bytes 1179648 | tf_op jit(solution)/shard_map/all_to_all | solution.py:229
  308.0 3.7 fusion.90
  314.4 6.7 %all-to-all-start.8 = ((bf16[16,24,768]{2,1,0:T(8,128)(2,1)}), bf16[16,24,768]{2,1,0:T(8,128)(2,1)}, u32[]{:S(2)}, u32[]{:S(2)}) async-start(bf16[16,24,768]{2,1,0:T(8,128)(2,1)} %bitcast.50), calls=%async_computation.8 | async-start | bytes 1179648 | tf_op jit(solution)/shard_map/all_to_all | solution.py:216
  325.1 10.1 %all-to-all-done.8 = bf16[16,24,768]{2,1,0:T(8,128)(2,1)} async-done(((bf16[16,24,768]{2,1,0:T(8,128)(2,1)}), bf16[16,24,768]{2,1,0:T(8,128)(2,1)}, u32[]{:S(2)}, u32[]{:S(2)}) %all-to-all-start.8) | async-done | bytes 589856 | tf_op jit(solution)/shard_map/all_to_all | solution.py:216
  335.2 4.8 broadcast_select_fusion.15
  340.0 2.8 convolution_convert_fusion.6
  342.8 4.8 all-to-all-start.9
  353.2 9.3 %all-to-all-done.9 = bf16[16,24,768]{2,1,0:T(8,128)(2,1)} async-done(((bf16[16,24,768]{2,1,0:T(8,128)(2,1)}), bf16[16,24,768]{2,1,0:T(8,128)(2,1)}, u32[]{:S(2)}, u32[]{:S(2)}) %all-to-all-start.9) | async-done | bytes 589856 | tf_op jit(solution)/shard_map/all_to_all | solution.py:229
  384.7 4.8 fusion.93
  389.5 3.4 add_convert_fusion.1
  392.9 5.3 %all-to-all-start.10 = ((bf16[16,48,1664]{2,1,0:T(8,128)(2,1)}), bf16[16,48,1664]{2,1,0:T(8,128)(2,1)S(1)}, u32[]{:S(2)}, u32[]{:S(2)}) async-start(bf16[16,48,1664]{2,1,0:T(8,128)(2,1)} %bitcast.247), calls=%async_computation.10 | async-start | bytes 5111808 | tf_op jit(solution)/shard_map/all_to_all | solution.py:343
  406.1 4.4 collective-permute-done.9
  412.5 43.3 %all-to-all-done.10 = bf16[16,48,1664]{2,1,0:T(8,128)(2,1)S(1)} async-done(((bf16[16,48,1664]{2,1,0:T(8,128)(2,1)}), bf16[16,48,1664]{2,1,0:T(8,128)(2,1)S(1)}, u32[]{:S(2)}, u32[]{:S(2)}) %all-to-all-start.10) | async-done | bytes 2555936 | tf_op jit(solution)/shard_map/all_to_all | solution.py:343
  455.9 4.5 all-to-all-start.11
  473.9 44.3 %all-to-all-done.11 = bf16[16,48,1664]{2,1,0:T(8,128)(2,1)} async-done(((bf16[16,48,1664]{2,1,0:T(8,128)(2,1)}), bf16[16,48,1664]{2,1,0:T(8,128)(2,1)}, u32[]{:S(2)}, u32[]{:S(2)}) %all-to-all-start.11) | async-done | bytes 2555936 | tf_op jit(solution)/shard_map/all_to_all | solution.py:343
  (439 shorter events, 135.6 us)
Async XLA Ops:
  3.2 1.8 collective-permute-start
  71.4 62.8 %all-to-all-start.3 = ((bf16[16,48,1664]{2,1,0:T(8,128)(2,1)}), bf16[16,48,1664]{2,1,0:T(8,128)(2,1)}, u32[]{:S(2)}, u32[]{:S(2)}) async-start(bf16[16,48,1664]{2,1,0:T(8,128)(2,1)} %broadcast_in_dim.71), calls=%async_computation.3 | async-start | bytes 5111808 | tf_op jit(solution)/shard_map/all_to_all | solution.py:336
  76.3 59.3 %collective-permute-start.1 = (bf16[768,1664]{1,0:T(8,128)(2,1)S(1)}, bf16[768,1664]{1,0:T(8,128)(2,1)}, u32[]{:S(2)}, u32[]{:S(2)}) collective-permute-start(bf16[768,1664]{1,0:T(8,128)(2,1)S(1)} %bitcast.245), channel_id=1, source_target_pairs={{0,16},{16,0},{1,17},{17,1},{2,18},{18,2},{3,19},{19,3},{4,20},{20... | collective-permute-start | bytes 7667720 | tf_op jit(solution)/shard_map/ppermute | solution.py:314
  79.0 4.3 collective-permute-start.2
  79.1 79.6 %collective-permute-start.3 = (bf16[768,768]{1,0:T(8,128)(2,1)}, bf16[768,768]{1,0:T(8,128)(2,1)}, u32[]{:S(2)}, u32[]{:S(2)}) collective-permute-start(bf16[768,768]{1,0:T(8,128)(2,1)} %bitcast.264), channel_id=1, source_target_pairs={{0,16},{16,0},{1,17},{17,1},{2,18},{18,2},{3,19},{19,3},{4,20},{20... | collective-permute-start | bytes 3538952 | tf_op jit(solution)/shard_map/ppermute | solution.py:314
  80.2 61.4 %copy-start.41 = (bf16[1,64,768]{2,1,0:T(8,128)(2,1)}, bf16[1,64,768]{2,1,0:T(8,128)(2,1)S(1)}, u32[]{:S(2)}) copy-start(bf16[1,64,768]{2,1,0:T(8,128)(2,1)S(1)} %get-tuple-element.79) | copy-start | bytes 294916
  80.2 61.3 %copy-start.104 = (f32[64]{0:T(128)}, f32[64]{0:T(128)S(1)}, u32[]{:S(2)}) copy-start(f32[64]{0:T(128)S(1)} %add_rsqrt_fusion.3) | copy-start | bytes 772
  81.8 64.1 %copy-start.21 = (pred[64,64,32]{1,2,0:T(32,128)(4,1)}, pred[64,64,32]{1,2,0:T(32,128)(4,1)S(1)}, u32[]{:S(2)}) copy-start(pred[64,64,32]{1,2,0:T(32,128)(4,1)S(1)} %copy.242) | copy-start | bytes 393220
  83.2 56.8 %copy-start.78 = (s32[64]{0:T(128)}, s32[64]{0:T(128)S(1)}, u32[]{:S(2)}) copy-start(s32[64]{0:T(128)S(1)} %get-tuple-element.107) | copy-start | bytes 772
  83.2 56.8 %copy-start.81 = (s32[64]{0:T(128)}, s32[64]{0:T(128)S(1)}, u32[]{:S(2)}) copy-start(s32[64]{0:T(128)S(1)} %get-tuple-element.106) | copy-start | bytes 772
  134.2 48.8 %collective-permute-start.5 = (bf16[768,1664]{1,0:T(8,128)(2,1)}, bf16[768,1664]{1,0:T(8,128)(2,1)}, u32[]{:S(2)}, u32[]{:S(2)}) collective-permute-start(bf16[768,1664]{1,0:T(8,128)(2,1)} %bitcast.24), channel_id=1, source_target_pairs={{0,16},{16,0},{1,17},{17,1},{2,18},{18,2},{3,19},{19,3},{4,20},{20... | collective-permute-start | bytes 7667720 | tf_op jit(solution)/shard_map/ppermute | solution.py:314
  140.1 52.4 %copy-start = (bf16[768,1664]{1,0:T(8,128)(2,1)}, bf16[768,1664]{1,0:T(8,128)(2,1)S(1)}, u32[]{:S(2)}) copy-start(bf16[768,1664]{1,0:T(8,128)(2,1)S(1)} %get-tuple-element.83) | copy-start | bytes 7667716
  151.2 49.2 %copy-start.8 = (f32[64,768]{1,0:T(8,128)}, f32[64,768]{1,0:T(8,128)S(1)}, u32[]{:S(2)}) copy-start(f32[64,768]{1,0:T(8,128)S(1)} %get-tuple-element.111) | copy-start | bytes 589828
  152.6 19.5 %all-to-all-start.1 = ((bf16[16,24,768]{2,1,0:T(8,128)(2,1)}), bf16[16,24,768]{2,1,0:T(8,128)(2,1)S(1)}, u32[]{:S(2)}, u32[]{:S(2)}) async-start(bf16[16,24,768]{2,1,0:T(8,128)(2,1)} %bitcast.253), calls=%async_computation.1 | async-start | bytes 1179648 | tf_op jit(solution)/shard_map/all_to_all | solution.py:142
  156.9 17.7 %collective-permute-start.4 = (bf16[768,768]{1,0:T(8,128)(2,1)}, bf16[768,768]{1,0:T(8,128)(2,1)}, u32[]{:S(2)}, u32[]{:S(2)}) collective-permute-start(bf16[768,768]{1,0:T(8,128)(2,1)} %bitcast.288), channel_id=1, source_target_pairs={{0,16},{16,0},{1,17},{17,1},{2,18},{18,2},{3,19},{19,3},{4,20},{20... | collective-permute-start | bytes 3538952 | tf_op jit(solution)/shard_map/ppermute | solution.py:314
  178.1 21.2 %all-to-all-start.2 = ((bf16[16,24,768]{2,1,0:T(8,128)(2,1)}), bf16[16,24,768]{2,1,0:T(8,128)(2,1)}, u32[]{:S(2)}, u32[]{:S(2)}) async-start(bf16[16,24,768]{2,1,0:T(8,128)(2,1)} %bitcast.21), calls=%async_computation.2 | async-start | bytes 1179648 | tf_op jit(solution)/shard_map/all_to_all | solution.py:151
  201.5 110.3 %copy-start.13 = (bf16[64,768]{1,0:T(8,128)(2,1)}, bf16[64,768]{1,0:T(8,128)(2,1)S(1)}, u32[]{:S(2)}) copy-start(bf16[64,768]{1,0:T(8,128)(2,1)S(1)} %get-tuple-element.75) | copy-start | bytes 294916
  233.7 17.0 %all-to-all-start.5 = ((bf16[16,24,768]{2,1,0:T(8,128)(2,1)}), bf16[16,24,768]{2,1,0:T(8,128)(2,1)S(1)}, u32[]{:S(2)}, u32[]{:S(2)}) async-start(bf16[16,24,768]{2,1,0:T(8,128)(2,1)} %bitcast.270), calls=%async_computation.5 | async-start | bytes 1179648 | tf_op jit(solution)/shard_map/all_to_all | solution.py:151
  314.4 20.8 %all-to-all-start.8 = ((bf16[16,24,768]{2,1,0:T(8,128)(2,1)}), bf16[16,24,768]{2,1,0:T(8,128)(2,1)}, u32[]{:S(2)}, u32[]{:S(2)}) async-start(bf16[16,24,768]{2,1,0:T(8,128)(2,1)} %bitcast.50), calls=%async_computation.8 | async-start | bytes 1179648 | tf_op jit(solution)/shard_map/all_to_all | solution.py:216
  342.8 19.7 %all-to-all-start.9 = ((bf16[16,24,768]{2,1,0:T(8,128)(2,1)}), bf16[16,24,768]{2,1,0:T(8,128)(2,1)}, u32[]{:S(2)}, u32[]{:S(2)}) async-start(bf16[16,24,768]{2,1,0:T(8,128)(2,1)} %bitcast.269), calls=%async_computation.9 | async-start | bytes 1179648 | tf_op jit(solution)/shard_map/all_to_all | solution.py:229
  351.1 38.4 %collective-permute-start.8 = (bf16[768,1664]{1,0:T(8,128)(2,1)}, bf16[768,1664]{1,0:T(8,128)(2,1)}, u32[]{:S(2)}, u32[]{:S(2)}) collective-permute-start(bf16[768,1664]{1,0:T(8,128)(2,1)} %broadcast_select_fusion.1), channel_id=1, source_target_pairs={{0,16},{16,0},{1,17},{17,1},{2,18},{18,2},{3,19},{19,3},{4,20},{20... | collective-permute-start | bytes 7667720 | tf_op jit(solution)/shard_map/ppermute | solution.py:314
  392.9 63.0 %all-to-all-start.10 = ((bf16[16,48,1664]{2,1,0:T(8,128)(2,1)}), bf16[16,48,1664]{2,1,0:T(8,128)(2,1)S(1)}, u32[]{:S(2)}, u32[]{:S(2)}) async-start(bf16[16,48,1664]{2,1,0:T(8,128)(2,1)} %bitcast.247), calls=%async_computation.10 | async-start | bytes 5111808 | tf_op jit(solution)/shard_map/all_to_all | solution.py:343
  403.9 6.6 %collective-permute-start.9 = (bf16[768,1664]{1,0:T(8,128)(2,1)S(1)}, bf16[768,1664]{1,0:T(8,128)(2,1)S(1)}, u32[]{:S(2)}, u32[]{:S(2)}) collective-permute-start(bf16[768,1664]{1,0:T(8,128)(2,1)S(1)} %broadcast_select_fusion), channel_id=1, source_target_pairs={{0,16},{16,0},{1,17},{17,1},{2,18},{18,2},{3,19},{19,3},{4,20},{20... | collective-permute-start | bytes 7667720 | tf_op jit(solution)/shard_map/ppermute | solution.py:314
  455.9 62.3 %all-to-all-start.11 = ((bf16[16,48,1664]{2,1,0:T(8,128)(2,1)}), bf16[16,48,1664]{2,1,0:T(8,128)(2,1)}, u32[]{:S(2)}, u32[]{:S(2)}) async-start(bf16[16,48,1664]{2,1,0:T(8,128)(2,1)} %bitcast.246), calls=%async_computation.11 | async-start | bytes 5111808 | tf_op jit(solution)/shard_map/all_to_all | solution.py:343
  461.7 5.3 %collective-permute-start.11 = (bf16[384,768]{1,0:T(8,128)(2,1)S(1)}, bf16[384,768]{1,0:T(8,128)(2,1)S(1)}, u32[]{:S(2)}, u32[]{:S(2)}) collective-permute-start(bf16[384,768]{1,0:T(8,128)(2,1)S(1)} %get-tuple-element.91), channel_id=1, source_target_pairs={{0,16},{16,0},{1,17},{17,1},{2,18},{18,2},{3,19},{19,3},{4,20},{20... | collective-permute-start | bytes 1769480 | tf_op jit(solution)/shard_map/ppermute | solution.py:314
  463.7 6.0 %collective-permute-start.13 = (bf16[384,768]{1,0:T(8,128)(2,1)S(1)}, bf16[384,768]{1,0:T(8,128)(2,1)S(1)}, u32[]{:S(2)}, u32[]{:S(2)}) collective-permute-start(bf16[384,768]{1,0:T(8,128)(2,1)S(1)} %copy-done.115), channel_id=1, source_target_pairs={{0,16},{16,0},{1,17},{17,1},{2,18},{18,2},{3,19},{19,3},{4,20},{20... | collective-permute-start | bytes 1769480 | tf_op jit(solution)/shard_map/ppermute | solution.py:314
  463.8 2.5 collective-permute-start.6
  464.2 2.9 collective-permute-start.12
  465.5 4.2 collective-permute-start.14
  473.1 48.7 %collective-permute-start.7 = (f32[64,768]{1,0:T(8,128)}, f32[64,768]{1,0:T(8,128)S(1)}, u32[]{:S(2)}, u32[]{:S(2)}) collective-permute-start(f32[64,768]{1,0:T(8,128)} %get-tuple-element.64), channel_id=1, source_target_pairs={{0,16},{16,0},{1,17},{17,1},{2,18},{18,2},{3,19},{19,3},{4,20},{20... | collective-permute-start | bytes 589832 | tf_op jit(solution)/shard_map/ppermute | solution.py:314
  473.9 48.0 %copy-start.52 = (f32[64,768]{1,0:T(8,128)S(1)}, f32[64,768]{1,0:T(8,128)}, u32[]{:S(2)}) copy-start(f32[64,768]{1,0:T(8,128)} %get-tuple-element.65) | copy-start | bytes 589828
  520.3 2.8 collective-permute-start.10
  (114 other events, 670.7 us)

commit v2 on v1

--- a/solution.py
+++ b/solution.py
@@ -4,6 +4,8 @@
 import jax.numpy as jnp
 import numpy as np
 from jax import lax
+from jax.experimental import pallas as pl
+from jax.experimental.pallas import tpu as pltpu
 from jax.sharding import PartitionSpec as P
 
 HEADS = 12
@@ -86,15 +88,235 @@
     return flat.reshape(expert_count, slot_count, row_count)
 
 
-def spread_copies(select, token_rows, dp_count):
-    expert_count = select.shape[0]
-    slot_count = select.shape[1]
-    model_width = token_rows.shape[1]
+MESH = pl.DeviceIdType.MESH
+
+
+def places_of(groups):
+    core = lax.axis_index("section")
+    me = lax.axis_index("dp")
+    group, place = me // SPLIT, lax.rem(me, SPLIT)
+    across = place + 1 - 2 * lax.rem(place, 2)
+    along = place + 2 - 4 * (place // 2)
+    return core, group, place, across, along, 3 - place
+
+
+def greet(targets):
+    barrier = pltpu.get_barrier_semaphore()
+    for target in targets:
+        pl.semaphore_signal(barrier, inc=1, device_id=target, device_id_type=MESH)
+    pl.semaphore_wait(barrier, len(targets))
+
+
+def send(source, landing, send_sem, recv_sem, target):
+    return pltpu.make_async_remote_copy(
+        src_ref=source,
+        dst_ref=landing,
+        send_sem=send_sem,
+        recv_sem=recv_sem,
+        device_id=target,
+        device_id_type=MESH,
+    )
+
+
+def spread_kernel(groups, both, src, out, send_sem, recv_sem, local_sem):
+    core, group, place, across, along, opposite = places_of(groups)
+    half = src.shape[-1] // 2
+
+    def device(member_group, member):
+        return (core, member_group * SPLIT + member)
+
+    def at(distance, member):
+        owner = lax.rem(group + groups - distance, groups) * SPLIT + member
+        return out.at[core, owner] if both else out.at[owner]
+
+    def part(block, which):
+        return block.at[:, pl.ds(which * half, half)]
+
+    side, line = device(group, across), device(group, along)
+    twin = (1 - core, group * SPLIT + place)
+    far = [lax.rem(group + k, groups) for k in range(groups)]
+    greet([side, line] + [device(far[k], place) for k in range(1, groups)] + ([twin] if both else []))
+    started = []
+
+    def go(source, landing, kind, distance, target):
+        copy = send(source, landing, send_sem.at[kind, distance], recv_sem.at[kind, distance], target)
+        copy.start()
+        started.append(copy)
+
+    def arrive(block, kind, distance, target):
+        send(block, block, send_sem.at[kind, distance], recv_sem.at[kind, distance], target).wait_recv()
+
+    def block_for(member_group):
+        return src if both else src.at[member_group]
+
+    own = block_for(group)
+    local = pltpu.make_async_copy(own, at(0, place), local_sem)
+    local.start()
+    go(own, at(0, place), 1, 0, side)
+    go(own, at(0, place), 2, 0, line)
+    for k in range(1, groups):
+        go(block_for(far[k]), at(0, place), 0, k, device(far[k], place))
+    if both:
+        go(own, at(0, place), 5, 0, twin)
+    for turn in range(groups + 2):
+        k = turn
+        if 0 < k < groups:
+            block = at(k, place)
+            arrive(block, 0, k, side)
+            go(block, block, 1, k, side)
+            go(block, block, 2, k, line)
+            if both:
+                go(block, block, 5, k, twin)
+        k = turn - 1
+        if 0 <= k < groups:
+            block = at(k, across)
+            arrive(block, 1, k, side)
+            go(part(block, 0), part(block, 0), 3, k, line)
+            if both:
+                go(block, block, 6, k, twin)
+            block = at(k, along)
+            arrive(block, 2, k, line)
+            go(part(block, 1), part(block, 1), 4, k, side)
+            if both:
+                go(block, block, 7, k, twin)
+        k = turn - 2
+        if 0 <= k < groups:
+            block = at(k, opposite)
+            arrive(part(block, 0), 3, k, line)
+            arrive(part(block, 1), 4, k, side)
+            if both:
+                go(block, block, 8, k, twin)
+    if both:
+        for kind, member in ((5, place), (6, across), (7, along), (8, opposite)):
+            for k in range(groups):
+                owner = lax.rem(group + groups - k, groups) * SPLIT + member
+                arrive(out.at[1 - core, owner], kind, k, twin)
+    local.wait()
+    for copy in started:
+        copy.wait_send()
+
+
+def spread(blocks, both, identity):
+    dp_count = lax.axis_size("dp")
+    groups = dp_count // SPLIT
+    shape = (dp_count,) + blocks.shape[-2:]
+    kinds = 9 if both else 5
+    return pl.pallas_call(
+        lambda *refs: spread_kernel(groups, both, *refs),
+        out_shape=jax.ShapeDtypeStruct(((2,) if both else ()) + shape, blocks.dtype),
+        in_specs=[pl.BlockSpec(memory_space=pl.ANY)],
+        out_specs=pl.BlockSpec(memory_space=pl.ANY),
+        scratch_shapes=[
+            pltpu.SemaphoreType.DMA((kinds, groups)),
+            pltpu.SemaphoreType.DMA((kinds, groups)),
+            pltpu.SemaphoreType.DMA,
+        ],
+        compiler_params=pltpu.CompilerParams(collective_id=identity, has_side_effects=True),
+    )(blocks)
+
+
+def collapse_kernel(groups, total, src, out, near, passed, pair, leaving, landed, send_sem, recv_sem):
+    core, group, place, across, along, opposite = places_of(groups)
+    half = src.shape[-1] // 2
+
+    def device(member_group, member):
+        return (core, member_group * SPLIT + member)
+
+    side, line = device(group, across), device(group, along)
+    far = [lax.rem(group + k, groups) for k in range(groups)]
+    back = [lax.rem(group + groups - k, groups) for k in range(groups)]
+    greet([side, line] + [device(far[k], place) for k in range(1, groups)])
+    order = list(range(1, groups)) + [0]
+    started = []
+
+    def copy_of(source, landing, kind, k, target):
+        return send(source, landing, send_sem.at[kind, k], recv_sem.at[kind, k], target)
+
+    def go(*parts):
+        copy = copy_of(*parts)
+        copy.start()
+        started.append(copy)
+
+    wide = jnp.float32
+    first, second = pl.ds(0, half), pl.ds(half, half)
+    for k in order:
+        block = src.at[far[k] * SPLIT + opposite]
+        go(block.at[:, first], near.at[0, k], 0, k, line)
+        go(block.at[:, second], near.at[1, k], 1, k, side)
+    for k in order:
+        index = far[k] * SPLIT + across
+        copy_of(near.at[0, k], near.at[0, k], 0, k, line).wait_recv()
+        passed[0, k, :, first] = (
+            src[index, :, first].astype(wide) + near[0, k].astype(wide)
+        ).astype(jnp.bfloat16)
+        passed[0, k, :, second] = src[index, :, second]
+        go(passed.at[0, k], pair.at[0, k], 2, k, side)
+        index = far[k] * SPLIT + along
+        copy_of(near.at[1, k], near.at[1, k], 1, k, side).wait_recv()
+        passed[1, k, :, second] = (
+            src[index, :, second].astype(wide) + near[1, k].astype(wide)
+        ).astype(jnp.bfloat16)
+        passed[1, k, :, first] = src[index, :, first]
+        go(passed.at[1, k], pair.at[1, k], 3, k, line)
+    for k in order:
+        copy_of(pair.at[0, k], pair.at[0, k], 2, k, side).wait_recv()
+        copy_of(pair.at[1, k], pair.at[1, k], 3, k, line).wait_recv()
+        whole = (
+            src[far[k] * SPLIT + place].astype(wide)
+            + pair[0, k].astype(wide)
+            + pair[1, k].astype(wide)
+        )
+        if k > 0:
+            leaving[k] = whole.astype(jnp.bfloat16)
+            go(leaving.at[k], landed.at[k], 4, k, device(far[k], place))
+        elif total:
+            out[...] = whole
+        else:
+            out[group] = whole.astype(jnp.bfloat16)
+    for k in range(1, groups):
+        copy_of(landed.at[k], landed.at[k], 4, k, side).wait_recv()
+        if total:
+            out[...] += landed[k].astype(wide)
+        else:
+            out[back[k]] = landed[k]
+    for copy in started:
+        copy.wait_send()
+
+
+def collapse(blocks, total, identity):
+    groups = blocks.shape[0] // SPLIT
+    rows, columns = blocks.shape[1:]
+    result = (
+        jax.ShapeDtypeStruct((rows, columns), jnp.float32)
+        if total
+        else jax.ShapeDtypeStruct((groups, rows, columns), blocks.dtype)
+    )
+    vmem = pl.BlockSpec(memory_space=pltpu.VMEM)
+    return pl.pallas_call(
+        lambda *refs: collapse_kernel(groups, total, *refs),
+        out_shape=result,
+        in_specs=[vmem],
+        out_specs=vmem,
+        scratch_shapes=[
+            pltpu.VMEM((2, groups, rows, columns // 2), blocks.dtype),
+            pltpu.VMEM((2, groups, rows, columns), blocks.dtype),
+            pltpu.VMEM((2, groups, rows, columns), blocks.dtype),
+            pltpu.VMEM((groups, rows, columns), blocks.dtype),
+            pltpu.VMEM((groups, rows, columns), blocks.dtype),
+            pltpu.SemaphoreType.DMA((5, groups)),
+            pltpu.SemaphoreType.DMA((5, groups)),
+        ],
+        compiler_params=pltpu.CompilerParams(
+            collective_id=identity, has_side_effects=True, vmem_limit_bytes=36 << 20
+        ),
+    )(blocks)
+
+
+def spread_copies(select, token_rows):
     grouped = jnp.einsum(
         "ect,td->ecd", select, token_rows, preferred_element_type=jnp.float32
     ).astype(jnp.bfloat16)
-    copies = jnp.broadcast_to(grouped[:, None], (expert_count, SPLIT, slot_count, model_width))
-    return copies.reshape(dp_count, slot_count, model_width)
+    return spread(grouped, False, 1)
 
 
 def rms_back(grad_rows, inputs, scale_rows):
@@ -138,8 +360,7 @@
     )
     gate_prob = jnp.sum(choice_prob * picked, axis=-1)
     select = placement_of(route_now, expert_count, slot_count)
-    outgoing = spread_copies(select, routed, dp_count)
-    arrived = lax.all_to_all(outgoing, "dp", split_axis=0, concat_axis=0, tiled=True)
+    arrived = spread_copies(select, routed)
     token_rows = arrived.reshape(-1, model_width)
     hidden = jnp.dot(token_rows, weight_in, preferred_element_type=jnp.float32)
     active = smooth(hidden).astype(jnp.bfloat16)
@@ -148,15 +369,11 @@
         .astype(jnp.bfloat16)
         .reshape(arrived.shape)
     )
-    coming_back = lax.all_to_all(partial_out, "dp", split_axis=0, concat_axis=0, tiled=True)
-    returned, hidden, arrived = (
-        coming_back,
-        hidden.reshape(arrived.shape[0], arrived.shape[1], -1),
-        arrived,
-    )
+    returned = collapse(partial_out, False, 2)
+    hidden = hidden.reshape(arrived.shape[0], arrived.shape[1], -1)
     combined = jnp.einsum(
-        "ekcd,ect->td",
-        returned.reshape(expert_count, SPLIT, slot_count, model_width),
+        "ecd,ect->td",
+        returned,
         select,
         preferred_element_type=jnp.float32,
     )
@@ -212,8 +429,7 @@
         jnp.bfloat16
     )
     routed_grad = jnp.einsum("te,de->td", logit_grad, w_route, preferred_element_type=jnp.float32)
-    outgoing = spread_copies(select, down_grad, dp_count)
-    arrived_grad = lax.all_to_all(outgoing, "dp", split_axis=0, concat_axis=0, tiled=True)
+    arrived_grad = spread_copies(select, down_grad)
     rows_grad = arrived_grad.reshape(-1, model_width)
     active_grad = jnp.einsum(
         "rd,fd->rf", rows_grad, weight_back, preferred_element_type=jnp.float32
@@ -226,16 +442,10 @@
     copy_grad = jnp.einsum(
         "rf,df->rd", hidden_grad, weight_in, preferred_element_type=jnp.float32
     ).astype(jnp.bfloat16)
-    copy_back = lax.all_to_all(
-        copy_grad.reshape(dp_count, slot_count, model_width),
-        "dp",
-        split_axis=0,
-        concat_axis=0,
-        tiled=True,
-    )
+    copy_back = collapse(copy_grad.reshape(dp_count, slot_count, model_width), False, 2)
     routed_grad = routed_grad + jnp.einsum(
-        "ekcd,ect->td",
-        copy_back.reshape(expert_count, SPLIT, slot_count, model_width),
+        "ecd,ect->td",
+        copy_back,
         select,
         preferred_element_type=jnp.float32,
     )
@@ -330,20 +540,6 @@
     return jnp.pad(table, ((0, 0), (0, row_share - table.shape[1]))).reshape(-1, 1)
 
 
-def gather_rows(shard):
-    dp_count = lax.axis_size("dp")
-    copies = jnp.broadcast_to(shard[None], (dp_count,) + shard.shape)
-    got = lax.all_to_all(copies, "dp", split_axis=0, concat_axis=0, tiled=True)
-    return got.reshape(dp_count * shard.shape[0], shard.shape[1])
-
-
-def sum_rows(whole):
-    dp_count = lax.axis_size("dp")
-    parts = whole.reshape(dp_count, whole.shape[0] // dp_count, whole.shape[1])
-    got = lax.all_to_all(parts, "dp", split_axis=0, concat_axis=0, tiled=True)
-    return jnp.sum(got.astype(jnp.float32), axis=0)
-
-
 def unpack_weights(packed, width, expert_count):
     dp_count = lax.axis_size("dp")
     small = packed[:, 4 * width :]
@@ -382,21 +578,11 @@
         attn_out[0],
         [norm_attn[0][:, None], norm_ffn[0][:, None], spaced(rel_bias[0], 1), router[0]],
     )
-    half = own_pack.shape[1] // 2
-    first_half, second_half = own_pack[:, :half], own_pack[:, half:]
-    other_part = swap_cores(per_core(core, second_half, first_half))
-    part_zero = per_core(core, first_half, other_part)
-    part_one = per_core(core, other_part, second_half)
-
-    def whole_of(part):
-        mine = gather_rows(part)
-        theirs = swap_cores(mine)
-        packed = jnp.concatenate(
-            [per_core(core, mine, theirs), per_core(core, theirs, mine)], axis=1
-        )
-        return unpack_weights(packed, width, expert_count)
-
-    weights = [whole_of(part_zero), None]
+    packs = spread(own_pack, True, 0)
+    weights = [
+        unpack_weights(packs[layer].reshape(width, own_pack.shape[1]), width, expert_count)
+        for layer in range(2)
+    ]
     other_in = swap_cores(expert_in[0, 0])
     other_out = swap_cores(expert_out[0, 0])
     ins = [per_core(core, expert_in[0, 0], other_in), per_core(core, other_in, expert_in[0, 0])]
@@ -413,7 +599,6 @@
     ]
     lengths = per_core(core, doc_lengths[0, 0], doc_lengths[1, 0])
     layer_in = per_core(core, tokens[0], tokens[1]).astype(jnp.float32)
-    weights[1] = whole_of(part_one)
     kept, lows = [], []
     for layer in range(2):
         result, state = layer_forward(
@@ -430,9 +615,10 @@
         return jnp.stack([per_core(core, mine, theirs), per_core(core, theirs, mine)])
 
     upstream = per_core(core, out_grad[0], out_grad[1]).astype(jnp.float32)
-    input_grads, expert_rows, summed = [None, None], [None, None], [None, None]
+    input_grads, expert_rows = [None, None], [None, None]
+    factors, smalls = [None, None], [None, None]
     for layer in (1, 0):
-        input_grad, small_grads, factor_rows, expert_rows[layer] = layer_backward(
+        input_grad, smalls[layer], factors[layer], expert_rows[layer] = layer_backward(
             upstream,
             kept[layer],
             weights[layer],
@@ -443,17 +629,31 @@
         )
         input_grads[layer] = input_grad
         upstream = input_grad.astype(jnp.bfloat16).astype(jnp.float32)
-        totals = shared_from(small_grads, factor_rows)
-        packed = pack_columns(
-            totals[1],
-            totals[3],
-            [totals[0][:, None], totals[4][:, None], spaced(totals[2], dp_count), totals[5]],
-        ).astype(jnp.bfloat16)
-        left, right = packed[:, :half], packed[:, half:]
-        theirs = swap_cores(per_core(core, right, left))
-        mine = per_core(core, left, right)
-        both = (mine.astype(jnp.float32) + theirs.astype(jnp.float32)).astype(jnp.bfloat16)
-        summed[layer] = sum_rows(both)
+
+    def own_layer(pair):
+        mine = per_core(core, pair[0], pair[1])
+        return mine, swap_cores(per_core(core, pair[1], pair[0]))
+
+    joined = own_layer([jnp.concatenate(group, axis=1) for group in factors])
+    joined = jnp.concatenate(joined, axis=0)
+    ends = np.cumsum([member.shape[1] for member in factors[0]])
+    factor_rows = [
+        joined[:, end - member.shape[1] : end] for end, member in zip(ends, factors[0])
+    ]
+    small_pair = own_layer([jnp.concatenate(group, axis=0) for group in smalls])
+    small_sum = small_pair[0] + small_pair[1]
+    small_grads = (
+        small_sum[:width],
+        small_sum[width:-width],
+        small_sum[-width:],
+    )
+    totals = shared_from(small_grads, factor_rows)
+    packed = pack_columns(
+        totals[1],
+        totals[3],
+        [totals[0][:, None], totals[4][:, None], spaced(totals[2], dp_count), totals[5]],
+    ).astype(jnp.bfloat16)
+    total = collapse(packed.reshape(dp_count, -1, packed.shape[1]), True, 3)
 
     def joined_rows(index):
         mine = per_core(core, expert_rows[0][index], expert_rows[1][index])
@@ -469,9 +669,6 @@
     )
     outputs = sorted_out(lows)
     input_store = sorted_out(input_grads)
-    mine = per_core(core, summed[0], summed[1])
-    theirs = swap_cores(per_core(core, summed[1], summed[0]))
-    total = jnp.concatenate([per_core(core, mine, theirs), per_core(core, theirs, mine)], axis=1)
     small = total[:, 4 * width :]
     return (
         outputs[None],

time: 536 us -> 361 us (0.67); the launches traced: 527 us -> 359 us
  Pallas kernels: 0 us -> 205 us
  waiting for transfers between devices: 192 us -> 0.03 us
  blocking collectives: 120 us -> 0 us
  starting transfers between devices: 54.8 us -> 30 us
  other arithmetic: 43 us -> 21.7 us
  local copies, waits for them, and re-layouts: 40.9 us -> 30.1 us
    pallas_call x0 -> x10, Pallas kernels: none -> 205 us  [the longest x5 111 us: spread(): pl.pallas_call(lambda *refs: spread_kernel(groups, both, *refs), out_shap...]
    all_to_all x8 -> x0, waiting for transfers between devices: 184 us -> none  [the longest x2 87.6 us: sum_rows(): got = lax.all_to_all(parts, 'dp', split_axis=0, concat_axis=0, tiled=True)]
    all_to_all x4 -> x0, blocking collectives: 120 us -> none  [the longest x1 63.4 us: gather_rows(): got = lax.all_to_all(copies, 'dp', split_axis=0, concat_axis=0, tiled=True)]
    all_to_all x8 -> x0, starting transfers between devices: 40.5 us -> none  [the longest x2 9.93 us: layer_forward(): lax.all_to_all(partial_out, 'dp', split_axis=0, concat_axis=0, tiled=True)]
    ppermute x15 -> x11, starting transfers between devices: 14.3 us -> 30 us  [swap_cores(): return lax.ppermute(block, 'section', [(0, 1), (1, 0)])]
    select_n x14 -> x8, other arithmetic: 17.1 us -> 5.4 us  [per_core(): return jnp.where(section_index == 0, first_one, second_one)]
    slice x2 -> x6, local copies, waits for them, and re-layouts: 0.45 us -> 9.44 us  [the longest x1 6.98 us: shards(): packs[layer].reshape(width, own_pack.shape[1])]
    ppermute x15 -> x11, waiting for transfers between devices: 7.83 us -> 0.03 us  [swap_cores(): return lax.ppermute(block, 'section', [(0, 1), (1, 0)])]
  transfers between devices with their start and end apart: 23 -> 11, of which waited for: 14 -> 0; matrix products, arithmetic and copies ran while one was open for 18% -> 16% of each run, Pallas kernels for 0% -> 21%
where the time goes in v2:
time: 361 us; the launch traced here: 359 us
  Pallas kernels  205 us (57%)
  matrix products  69.9 us (19%)
  local copies, waits for them, and re-layouts  30.1 us (8%)
  starting transfers between devices  30 us (8%)
  other arithmetic  21.7 us (6%)
    pallas_call x5, Pallas kernels, spread(): pl.pallas_call(lambda *refs: spread_kernel(groups, both, *refs), out_shap...  111 us
    pallas_call x5, Pallas kernels, collapse(): pl.pallas_call(lambda *refs: collapse_kernel(groups, total, *refs), out_s...  94 us
    ppermute x11, starting transfers between devices, swap_cores(): return lax.ppermute(block, 'section', [(0, 1), (1, 0)])  30 us
    dot_general x2, matrix products, layer_backward(): jnp.einsum('rd,fd->rf', rows_grad, weight_back, preferred_element_type=jn...  7.75 us
    unnamed x194, local copies, waits for them, and re-layouts  7.35 us
    dot_general x2, matrix products, layer_backward(): jnp.einsum('te,de->td', qkv_grad, w_qkv, preferred_element_type=jnp.float32)  7.27 us
  transfers between devices with their start and end apart: 11, of which 0 were waited for; matrix products, arithmetic and copies ran while one was open for 16% of the time, Pallas kernels for 21%

profile of v2, /device:TPU:13, one launch (start us, length us, event | category | flops | bytes accessed | tf_op | source)
XLA Modules:
  0.0 359.2 jit_solution(13222896187543172901)
XLA Ops:
  5.1 1.7 fusion.63.refs_0_
  6.8 51.1 %shard_map.204 = bf16[2,16,48,3328]{3,2,1,0:T(8,128)(2,1)} custom-call(bf16[48,3328]{1,0:T(8,128)(2,1)} %fusion.63.refs_0_), custom_call_target="tpu_custom_call" | custom-call | tf_op jit(solution)/shard_map/pallas_call | solution.py:204
  58.0 7.0 %fusion.202 = (bf16[1,16,48,3328]{3,2,1,0:T(8,128)(2,1)}, bf16[1,16,48,3328]{3,2,1,0:T(8,128)(2,1)S(1)}) fusion(bf16[2,16,48,3328]{3,2,1,0:T(8,128)(2,1)} %shard_map.204), kind=kLoop, calls=%fused_computation.366 | loop fusion | bytes 20447232 | tf_op jit(solution)/shard_map/slice | solution.py:583
  65.0 2.4 fusion.101
  69.5 2.9 convolution_convert_fusion.2
  78.2 1.8 multiply_reduce_fusion.7
  86.6 22.9 %shard_map.205 = bf16[16,24,768]{2,1,0:T(8,128)(2,1)} custom-call(bf16[4,24,768]{2,1,0:T(8,128)(2,1)} %convolution_convert_fusion.15.refs_0_), custom_call_target="tpu_custom_call" | custom-call | tf_op jit(solution)/shard_map/pallas_call | solution.py:204
  109.8 2.6 fusion.59
  112.5 2.9 convolution_convert_fusion.7
  115.4 8.8 %shard_map.206 = bf16[4,24,768]{2,1,0:T(8,128)(2,1)S(1)} custom-call(bf16[16,24,768]{2,1,0:T(8,128)(2,1)S(1)} %bitcast.220), custom_call_target="tpu_custom_call" | custom-call | tf_op jit(solution)/shard_map/pallas_call | solution.py:295
  129.7 1.8 multiply_reduce_fusion.6
  134.2 12.6 %shard_map.207 = bf16[16,24,768]{2,1,0:T(8,128)(2,1)} custom-call(bf16[4,24,768]{2,1,0:T(8,128)(2,1)} %convolution_convert_fusion.14.refs_0_), custom_call_target="tpu_custom_call" | custom-call | tf_op jit(solution)/shard_map/pallas_call | solution.py:204
  146.9 4.1 %broadcast_select_fusion.9 = (bf16[384,768]{1,0:T(8,128)(2,1)}, bf16[384,768]{1,0:T(8,128)(2,1)}, f32[384,768]{1,0:T(8,128)S(1)}) fusion(pred[]{:T(512)S(6)} %eq.70, f32[384,768]{1,0:T(8,128)} %copy-done.9, bf16[384,768]{1,0:T(8,128)(2,1)} %bitcast.244, bf16[768,768]{1,0:T(8,128)(2,1)} %collective-permute-done.1, bf16[1,1,768,768]{3,2,1,0:T(8,128)(2,1)} %param.23), kind=kOutput, calls=%fused_computation.119 | convolution fusion | flops 459472896 | bytes 6488065 | tf_op jit(solution)/shard_map/dot_general | solution.py:365
  152.1 9.7 %shard_map.208 = bf16[4,24,768]{2,1,0:T(8,128)(2,1)S(1)} custom-call(bf16[16,24,768]{2,1,0:T(8,128)(2,1)S(1)} %bitcast.221), custom_call_target="tpu_custom_call" | custom-call | tf_op jit(solution)/shard_map/pallas_call | solution.py:295
  163.8 12.7 %shard_map.209 = bf16[16,24,768]{2,1,0:T(8,128)(2,1)} custom-call(bf16[4,24,768]{2,1,0:T(8,128)(2,1)} %convolution_convert_fusion.13.refs_0_), custom_call_target="tpu_custom_call" | custom-call | tf_op jit(solution)/shard_map/pallas_call | solution.py:204
  176.5 3.1 fusion.29
  180.4 11.1 %shard_map.210 = bf16[4,24,768]{2,1,0:T(8,128)(2,1)S(1)} custom-call(bf16[16,24,768]{2,1,0:T(8,128)(2,1)S(1)} %bitcast.222), custom_call_target="tpu_custom_call" | custom-call | tf_op jit(solution)/shard_map/pallas_call | solution.py:295
  191.8 1.8 multiply_reduce_fusion.2
  193.8 1.8 convolution_convert_fusion.17
  200.3 3.9 %fusion.100 = (f32[768]{0:T(1024)}, f32[64]{0:T(128)S(1)}, f32[64,768]{1,0:T(8,128)S(1)}) fusion(bf16[64,768]{1,0:T(8,128)(2,1)S(1)} %get-tuple-element.69, f32[64]{0:T(128)S(1)} %copy-done.77, f32[768]{0:T(1024)S(1)} %convert_reduce_fusion.4, bf16[768,3328]{1,0:T(8,128)(2,1)} %bitcast.236, bf16[64,768]{1,0:T(8,128)(2,1)S(1)} %copy.266, ...), kind=kOutput, calls=%fused_computation.185 | convolution fusion | flops 227769536 | bytes 4135424 | tf_op jit(solution)/shard_map/te,de->td/dot_general | solution.py:490
  205.4 11.7 %shard_map.211 = bf16[16,24,768]{2,1,0:T(8,128)(2,1)} custom-call(bf16[4,24,768]{2,1,0:T(8,128)(2,1)} %convolution_convert_fusion.12.refs_0_), custom_call_target="tpu_custom_call" | custom-call | tf_op jit(solution)/shard_map/pallas_call | solution.py:204
  217.1 4.7 %broadcast_select_fusion.11 = (bf16[384,768]{1,0:T(8,128)(2,1)}, bf16[384,768]{1,0:T(8,128)(2,1)}, bf16[384,768]{1,0:T(8,128)(2,1)S(1)}) fusion(bf16[384,768]{1,0:T(8,128)(2,1)S(1)} %copy-done.84, pred[]{:T(512)S(6)} %eq.70, f32[384,768]{1,0:T(8,128)} %copy-done.9, bf16[384,768]{1,0:T(8,128)(2,1)} %bitcast.243, ...), kind=kOutput, calls=%fused_computation.121 | convolution fusion | flops 460062720 | bytes 6488065 | tf_op jit(solution)/shard_map/rd,fd->rf/dot_general | solution.py:434
  221.8 2.0 convolution_convert_fusion.4
  223.8 10.5 %shard_map.212 = bf16[4,24,768]{2,1,0:T(8,128)(2,1)S(1)} custom-call(bf16[16,24,768]{2,1,0:T(8,128)(2,1)S(1)} %bitcast.219), custom_call_target="tpu_custom_call" | custom-call | tf_op jit(solution)/shard_map/pallas_call | solution.py:295
  236.1 1.8 convolution_convert_fusion.16
  238.0 2.0 convolution_convert_fusion.8
  240.9 1.7 copy.265
  245.8 26.6 %collective-permute-start.3 = (bf16[64,768]{1,0:T(8,128)(2,1)}, bf16[64,768]{1,0:T(8,128)(2,1)}, u32[]{:S(2)}, u32[]{:S(2)}) collective-permute-start(bf16[64,768]{1,0:T(8,128)(2,1)} %get-tuple-element.66), channel_id=1, source_target_pairs={{0,16},{16,0},{1,17},{17,1},{2,18},{18,2},{3,19},{19,3},{4,20},{20... | collective-permute-start | bytes 294920 | tf_op jit(solution)/shard_map/ppermute | solution.py:524
  273.8 3.4 fusion.103
  291.7 3.9 %convolution_bitcast_fusion.1 = f32[1,1,768,768]{3,2,1,0:T(8,128)} fusion(bf16[384,768]{1,0:T(8,128)(2,1)} %collective-permute-done.7, bf16[384,768]{1,0:T(8,128)(2,1)S(1)} %copy-done.16, bf16[384,768]{1,0:T(8,128)(2,1)} %collective-permute-done.8, bf16[384,768]{1,0:T(8,128)(2,1)S(1)} %copy-done.87), kind=kOutput, calls=%fused_computation.25 | convolution fusion | flops 910688256 | bytes 4718592 | tf_op jit(solution)/shard_map/rd,rf->df/dot_general | solution.py:664
  295.6 3.6 convolution_bitcast_fusion
  301.7 53.9 %shard_map.213 = f32[48,3328]{1,0:T(8,128)S(1)} custom-call(bf16[16,48,3328]{2,1,0:T(8,128)(2,1)S(1)} %pad_maximum_fusion.refs_0_), custom_call_target="tpu_custom_call" | custom-call | tf_op jit(solution)/shard_map/pallas_call | solution.py:295
  (358 shorter events, 64.2 us)
Async XLA Ops:
  1.8 83.6 %collective-permute-start = (s32[64]{0:T(128)}, s32[64]{0:T(128)S(1)}, u32[]{:S(2)}, u32[]{:S(2)}) collective-permute-start(s32[64]{0:T(128)} %fusion.183), channel_id=1, source_target_pairs={{0,16},{16,0},{1,17},{17,1},{2,18},{18,2},{3,19},{19,3},{4,20},{20... | collective-permute-start | bytes 776 | tf_op jit(solution)/shard_map/ppermute | solution.py:524
  2.5 109.9 %collective-permute-start.2 = (bf16[768,768]{1,0:T(8,128)(2,1)}, bf16[768,768]{1,0:T(8,128)(2,1)}, u32[]{:S(2)}, u32[]{:S(2)}) collective-permute-start(bf16[768,768]{1,0:T(8,128)(2,1)} %bitcast.275), channel_id=1, source_target_pairs={{0,16},{16,0},{1,17},{17,1},{2,18},{18,2},{3,19},{19,3},{4,20},{20... | collective-permute-start | bytes 3538952 | tf_op jit(solution)/shard_map/ppermute | solution.py:524
  2.5 107.3 %collective-permute-start.1 = (bf16[768,768]{1,0:T(8,128)(2,1)}, bf16[768,768]{1,0:T(8,128)(2,1)}, u32[]{:S(2)}, u32[]{:S(2)}) collective-permute-start(bf16[768,768]{1,0:T(8,128)(2,1)} %bitcast.254), channel_id=1, source_target_pairs={{0,16},{16,0},{1,17},{17,1},{2,18},{18,2},{3,19},{19,3},{4,20},{20... | collective-permute-start | bytes 3538952 | tf_op jit(solution)/shard_map/ppermute | solution.py:524
  81.9 27.6 %copy-start.51 = (f32[64]{0:T(128)}, f32[64]{0:T(128)S(1)}, u32[]{:S(2)}) copy-start(f32[64]{0:T(128)S(1)} %get-tuple-element.109) | copy-start | bytes 772
  84.4 28.0 %copy-start.62 = (f32[64]{0:T(128)}, f32[64]{0:T(128)S(1)}, u32[]{:S(2)}) copy-start(f32[64]{0:T(128)S(1)} %fusion.154) | copy-start | bytes 772
  85.5 26.9 %copy-start.41 = (s32[64]{0:T(128)}, s32[64]{0:T(128)S(1)}, u32[]{:S(2)}) copy-start(s32[64]{0:T(128)S(1)} %get-tuple-element.104) | copy-start | bytes 772
  85.5 106.3 %copy-start.44 = (s32[64]{0:T(128)}, s32[64]{0:T(128)S(1)}, u32[]{:S(2)}) copy-start(s32[64]{0:T(128)S(1)} %get-tuple-element.103) | copy-start | bytes 772
  85.7 38.6 %copy-start.67 = (s32[64]{0:T(128)}, s32[64]{0:T(128)S(1)}, u32[]{:S(2)}) copy-start(s32[64]{0:T(128)S(1)} %multiply_add_fusion.2) | copy-start | bytes 772
  109.7 14.5 %copy-start.56 = (f32[64]{0:T(128)}, f32[64]{0:T(128)S(1)}, u32[]{:S(2)}) copy-start(f32[64]{0:T(128)S(1)} %select_reduce_fusion.1) | copy-start | bytes 772
  109.8 15.6 %slice-start = ((s8[5111808]{0:T(1024)(128)(4,1)}), s8[4194304]{0:T(1024)(128)(4,1)S(1)}, s32[]{:S(2)}) async-start(s8[5111808]{0:T(1024)(128)(4,1)} %bitcast.237), calls=%async_computation | async-start | bytes 8388608
  112.4 13.0 %slice-start.1 = ((s8[5111808]{0:T(1024)(128)(4,1)}), s8[917504]{0:T(1024)(128)(4,1)S(1)}, s32[]{:S(2)}) async-start(s8[5111808]{0:T(1024)(128)(4,1)} %bitcast.237), calls=%async_computation.1 | async-start | bytes 1835008
  131.5 62.2 %copy-start.69 = (f32[64]{0:T(128)}, f32[64]{0:T(128)S(1)}, u32[]{:S(2)}) copy-start(f32[64]{0:T(128)S(1)} %add_rsqrt_fusion) | copy-start | bytes 772
  132.8 59.0 %copy-start.54 = (f32[64]{0:T(128)}, f32[64]{0:T(128)S(1)}, u32[]{:S(2)}) copy-start(f32[64]{0:T(128)S(1)} %get-tuple-element.116) | copy-start | bytes 772
  133.1 58.7 %copy-start.65 = (f32[64]{0:T(128)}, f32[64]{0:T(128)S(1)}, u32[]{:S(2)}) copy-start(f32[64]{0:T(128)S(1)} %fusion.156) | copy-start | bytes 772
  133.3 58.5 %copy-start.49 = (f32[64]{0:T(128)}, f32[64]{0:T(128)S(1)}, u32[]{:S(2)}) copy-start(f32[64]{0:T(128)S(1)} %select_reduce_fusion) | copy-start | bytes 772
  162.9 28.9 %copy-start.73 = (f32[64]{0:T(128)}, f32[64]{0:T(128)S(1)}, u32[]{:S(2)}) copy-start(f32[64]{0:T(128)S(1)} %get-tuple-element.64) | copy-start | bytes 772
  204.2 12.9 %copy-start.84 = (bf16[384,768]{1,0:T(8,128)(2,1)S(1)}, bf16[384,768]{1,0:T(8,128)(2,1)}, u32[]{:S(2)}) copy-start(bf16[384,768]{1,0:T(8,128)(2,1)} %copy-done.83) | copy-start | bytes 1769476
  204.4 30.1 %copy-start.71 = (f32[64]{0:T(128)}, f32[64]{0:T(128)S(1)}, u32[]{:S(2)}) copy-start(f32[64]{0:T(128)S(1)} %get-tuple-element.62) | copy-start | bytes 772
  221.7 12.8 %copy-start.52 = (f32[64]{0:T(128)S(1)}, f32[64]{0:T(128)}, u32[]{:S(2)}) copy-start(f32[64]{0:T(128)} %copy-done.51) | copy-start | bytes 772
  221.8 12.8 %copy-start.60 = (f32[64]{0:T(128)S(1)}, f32[64]{0:T(128)}, u32[]{:S(2)}) copy-start(f32[64]{0:T(128)} %copy-done.59) | copy-start | bytes 772
  221.8 12.8 %copy-start.63 = (f32[64]{0:T(128)S(1)}, f32[64]{0:T(128)}, u32[]{:S(2)}) copy-start(f32[64]{0:T(128)} %copy-done.62) | copy-start | bytes 772
  244.6 27.8 %copy-start.30 = (bf16[12,64,64]{2,1,0:T(8,128)(2,1)S(1)}, bf16[12,64,64]{2,1,0:T(8,128)(2,1)}, u32[]{:S(2)}) copy-start(bf16[12,64,64]{2,1,0:T(8,128)(2,1)} %convolution_convert_fusion.8) | copy-start | bytes 294916
  245.8 28.0 %copy-start.37 = (f32[768]{0:T(1024)S(1)}, f32[768]{0:T(1024)}, u32[]{:S(2)}) copy-start(f32[768]{0:T(1024)} %copy-done.36) | copy-start | bytes 9220
  245.8 28.0 %copy-start.79 = (f32[64]{0:T(128)S(1)}, f32[64]{0:T(128)}, u32[]{:S(2)}) copy-start(f32[64]{0:T(128)} %copy-done.78) | copy-start | bytes 772
  245.8 42.0 %collective-permute-start.3 = (bf16[64,768]{1,0:T(8,128)(2,1)}, bf16[64,768]{1,0:T(8,128)(2,1)}, u32[]{:S(2)}, u32[]{:S(2)}) collective-permute-start(bf16[64,768]{1,0:T(8,128)(2,1)} %get-tuple-element.66), channel_id=1, source_target_pairs={{0,16},{16,0},{1,17},{17,1},{2,18},{18,2},{3,19},{19,3},{4,20},{20... | collective-permute-start | bytes 294920 | tf_op jit(solution)/shard_map/ppermute | solution.py:524
  278.1 11.3 %collective-permute-start.4 = (f32[64,768]{1,0:T(8,128)}, f32[64,768]{1,0:T(8,128)}, u32[]{:S(2)}, u32[]{:S(2)}) collective-permute-start(f32[64,768]{1,0:T(8,128)} %get-tuple-element.60), channel_id=1, source_target_pairs={{0,16},{16,0},{1,17},{17,1},{2,18},{18,2},{3,19},{19,3},{4,20},{20... | collective-permute-start | bytes 589832 | tf_op jit(solution)/shard_map/ppermute | solution.py:524
  283.6 3.3 collective-permute-start.6
  284.2 7.5 %collective-permute-start.7 = (bf16[384,768]{1,0:T(8,128)(2,1)}, bf16[384,768]{1,0:T(8,128)(2,1)}, u32[]{:S(2)}, u32[]{:S(2)}) collective-permute-start(bf16[384,768]{1,0:T(8,128)(2,1)} %get-tuple-element.89), channel_id=1, source_target_pairs={{0,16},{16,0},{1,17},{17,1},{2,18},{18,2},{3,19},{19,3},{4,20},{20... | collective-permute-start | bytes 1769480 | tf_op jit(solution)/shard_map/ppermute | solution.py:524
  284.3 7.4 %collective-permute-start.8 = (bf16[384,768]{1,0:T(8,128)(2,1)}, bf16[384,768]{1,0:T(8,128)(2,1)}, u32[]{:S(2)}, u32[]{:S(2)}) collective-permute-start(bf16[384,768]{1,0:T(8,128)(2,1)} %get-tuple-element.87), channel_id=1, source_target_pairs={{0,16},{16,0},{1,17},{17,1},{2,18},{18,2},{3,19},{19,3},{4,20},{20... | collective-permute-start | bytes 1769480 | tf_op jit(solution)/shard_map/ppermute | solution.py:524
  286.9 8.6 %collective-permute-start.9 = (bf16[384,768]{1,0:T(8,128)(2,1)}, bf16[384,768]{1,0:T(8,128)(2,1)}, u32[]{:S(2)}, u32[]{:S(2)}) collective-permute-start(bf16[384,768]{1,0:T(8,128)(2,1)} %get-tuple-element.81), channel_id=1, source_target_pairs={{0,16},{16,0},{1,17},{17,1},{2,18},{18,2},{3,19},{19,3},{4,20},{20... | collective-permute-start | bytes 1769480 | tf_op jit(solution)/shard_map/ppermute | solution.py:524
  287.7 7.9 %collective-permute-start.10 = (bf16[384,768]{1,0:T(8,128)(2,1)}, bf16[384,768]{1,0:T(8,128)(2,1)S(1)}, u32[]{:S(2)}, u32[]{:S(2)}) collective-permute-start(bf16[384,768]{1,0:T(8,128)(2,1)} %get-tuple-element.85), channel_id=1, source_target_pairs={{0,16},{16,0},{1,17},{17,1},{2,18},{18,2},{3,19},{19,3},{4,20},{20... | collective-permute-start | bytes 1769480 | tf_op jit(solution)/shard_map/ppermute | solution.py:524
  289.4 9.8 %collective-permute-start.5 = (bf16[64,5380]{1,0:T(8,128)(2,1)S(1)}, bf16[64,5380]{1,0:T(8,128)(2,1)S(1)}, u32[]{:S(2)}, u32[]{:S(2)}) collective-permute-start(bf16[64,5380]{1,0:T(8,128)(2,1)S(1)} %copy-done.15), channel_id=1, source_target_pairs={{0,16},{16,0},{1,17},{17,1},{2,18},{18,2},{3,19},{19,3},{4,20},{20... | collective-permute-start | bytes 2065928 | tf_op jit(solution)/shard_map/ppermute | solution.py:524
  (69 other events, 242.8 us)

commit v3 on v2

--- a/solution.py
+++ b/solution.py
@@ -201,11 +201,12 @@
     groups = dp_count // SPLIT
     shape = (dp_count,) + blocks.shape[-2:]
     kinds = 9 if both else 5
+    space = pl.BlockSpec(memory_space=pl.ANY if both else pltpu.VMEM)
     return pl.pallas_call(
         lambda *refs: spread_kernel(groups, both, *refs),
         out_shape=jax.ShapeDtypeStruct(((2,) if both else ()) + shape, blocks.dtype),
-        in_specs=[pl.BlockSpec(memory_space=pl.ANY)],
-        out_specs=pl.BlockSpec(memory_space=pl.ANY),
+        in_specs=[space],
+        out_specs=space,
         scratch_shapes=[
             pltpu.SemaphoreType.DMA((kinds, groups)),
             pltpu.SemaphoreType.DMA((kinds, groups)),
@@ -312,11 +313,10 @@
     )(blocks)
 
 
-def spread_copies(select, token_rows):
-    grouped = jnp.einsum(
+def grouped_rows(select, token_rows):
+    return jnp.einsum(
         "ect,td->ecd", select, token_rows, preferred_element_type=jnp.float32
     ).astype(jnp.bfloat16)
-    return spread(grouped, False, 1)
 
 
 def rms_back(grad_rows, inputs, scale_rows):
@@ -330,7 +330,19 @@
     return jax.nn.gelu(values, approximate=True)
 
 
-def layer_forward(layer_in, weights, route_now, lengths, weight_in, weight_back):
+def expert_pull(hidden_rows, rows_grad, weight_in, weight_back):
+    active_grad = jnp.einsum(
+        "rd,fd->rf", rows_grad, weight_back, preferred_element_type=jnp.float32
+    )
+    smooth_pull = jax.vjp(smooth, hidden_rows)[1]
+    hidden_grad = smooth_pull(active_grad)[0].astype(jnp.bfloat16)
+    copy_grad = jnp.einsum(
+        "rf,df->rd", hidden_grad, weight_in, preferred_element_type=jnp.float32
+    ).astype(jnp.bfloat16)
+    return hidden_grad, copy_grad
+
+
+def layer_forward(layer_in, weights, route_now, lengths, weight_in, weight_back, upstream=None):
     gain_one, w_qkv, table, w_out, gain_two, w_route = weights
     row_count, model_width = layer_in.shape
     dp_count = lax.axis_size("dp")
@@ -360,7 +372,15 @@
     )
     gate_prob = jnp.sum(choice_prob * picked, axis=-1)
     select = placement_of(route_now, expert_count, slot_count)
-    arrived = spread_copies(select, routed)
+    grouped = grouped_rows(select, routed)
+    if upstream is None:
+        arrived = spread(grouped, False, 1)
+    else:
+        down_grad = (gate_prob[:, None] * upstream).astype(jnp.bfloat16)
+        grouped = jnp.concatenate([grouped, grouped_rows(select, down_grad)], axis=1)
+        arrived_both = spread(grouped, False, 4)
+        arrived = arrived_both[:, :slot_count]
+        rows_grad = arrived_both[:, slot_count:].reshape(-1, model_width)
     token_rows = arrived.reshape(-1, model_width)
     hidden = jnp.dot(token_rows, weight_in, preferred_element_type=jnp.float32)
     active = smooth(hidden).astype(jnp.bfloat16)
@@ -369,7 +389,15 @@
         .astype(jnp.bfloat16)
         .reshape(arrived.shape)
     )
-    returned = collapse(partial_out, False, 2)
+    if upstream is None:
+        returned = collapse(partial_out, False, 2)
+        early = None
+    else:
+        hidden_grad, copy_grad = expert_pull(hidden, rows_grad, weight_in, weight_back)
+        leaving = jnp.concatenate([partial_out, copy_grad.reshape(arrived.shape)], axis=1)
+        coming = collapse(leaving, False, 5)
+        returned = coming[:, :slot_count]
+        early = (rows_grad, hidden_grad, coming[:, slot_count:])
     hidden = hidden.reshape(arrived.shape[0], arrived.shape[1], -1)
     combined = jnp.einsum(
         "ecd,ect->td",
@@ -391,8 +419,10 @@
         choice_prob,
         gate_prob,
         combined,
+        active,
         hidden,
         arrived,
+        early,
     )
     return (result, kept_state)
 
@@ -411,8 +441,10 @@
         choice_prob,
         gate_prob,
         combined,
+        active,
         hidden,
         arrived,
+        early,
     ) = kept_state
     gain_one, w_qkv, table, w_out, gain_two, w_route = weights
     row_count, model_width = layer_in.shape
@@ -423,26 +455,20 @@
         jnp.float32
     )
     select = placement_of(route_now, expert_count, slot_count)
-    down_grad = (gate_prob[:, None] * upstream).astype(jnp.bfloat16)
     gate_grad = jnp.sum(upstream * combined, axis=-1)
     logit_grad = (choice_prob * (picked - gate_prob[:, None]) * gate_grad[:, None]).astype(
         jnp.bfloat16
     )
     routed_grad = jnp.einsum("te,de->td", logit_grad, w_route, preferred_element_type=jnp.float32)
-    arrived_grad = spread_copies(select, down_grad)
-    rows_grad = arrived_grad.reshape(-1, model_width)
-    active_grad = jnp.einsum(
-        "rd,fd->rf", rows_grad, weight_back, preferred_element_type=jnp.float32
-    )
-    hidden_rows = hidden.reshape(rows_grad.shape[0], -1)
-    active_rows, smooth_pull = jax.vjp(smooth, hidden_rows)
-    hidden_grad = smooth_pull(active_grad)[0].astype(jnp.bfloat16)
-    active_low = active_rows.astype(jnp.bfloat16)
+    if early is None:
+        down_grad = (gate_prob[:, None] * upstream).astype(jnp.bfloat16)
+        rows_grad = spread(grouped_rows(select, down_grad), False, 1).reshape(-1, model_width)
+        hidden_rows = hidden.reshape(rows_grad.shape[0], -1)
+        hidden_grad, copy_grad = expert_pull(hidden_rows, rows_grad, weight_in, weight_back)
+        copy_back = collapse(copy_grad.reshape(dp_count, slot_count, model_width), False, 2)
+    else:
+        rows_grad, hidden_grad, copy_back = early
     arrived_rows = arrived.reshape(-1, model_width)
-    copy_grad = jnp.einsum(
-        "rf,df->rd", hidden_grad, weight_in, preferred_element_type=jnp.float32
-    ).astype(jnp.bfloat16)
-    copy_back = collapse(copy_grad.reshape(dp_count, slot_count, model_width), False, 2)
     routed_grad = routed_grad + jnp.einsum(
         "ecd,ect->td",
         copy_back,
@@ -494,7 +520,7 @@
     )
     small_grads = (gain_one_grad, table_grad, gain_two_grad)
     factor_rows = (normed, qkv_grad, attended, branch_grad, routed, logit_grad)
-    expert_rows = (arrived_rows, hidden_grad, active_low, rows_grad)
+    expert_rows = (arrived_rows, hidden_grad, active, rows_grad)
     return (input_grad, small_grads, factor_rows, expert_rows)
 
 
@@ -599,10 +625,17 @@
     ]
     lengths = per_core(core, doc_lengths[0, 0], doc_lengths[1, 0])
     layer_in = per_core(core, tokens[0], tokens[1]).astype(jnp.float32)
+    upstream = per_core(core, out_grad[0], out_grad[1]).astype(jnp.float32)
     kept, lows = [], []
     for layer in range(2):
         result, state = layer_forward(
-            layer_in, weights[layer], route_rows[layer], lengths, ins[layer], outs[layer]
+            layer_in,
+            weights[layer],
+            route_rows[layer],
+            lengths,
+            ins[layer],
+            outs[layer],
+            upstream if layer == 1 else None,
         )
         low = result.astype(jnp.bfloat16)
         lows.append(low)
@@ -614,7 +647,6 @@
         theirs = swap_cores(per_core(core, pair[1], pair[0]))
         return jnp.stack([per_core(core, mine, theirs), per_core(core, theirs, mine)])
 
-    upstream = per_core(core, out_grad[0], out_grad[1]).astype(jnp.float32)
     input_grads, expert_rows = [None, None], [None, None]
     factors, smalls = [None, None], [None, None]
     for layer in (1, 0):
@@ -656,8 +688,11 @@
     total = collapse(packed.reshape(dp_count, -1, packed.shape[1]), True, 3)
 
     def joined_rows(index):
-        mine = per_core(core, expert_rows[0][index], expert_rows[1][index])
-        theirs = swap_cores(per_core(core, expert_rows[1][index], expert_rows[0][index]))
+        first_one, second_one = expert_rows[0][index], expert_rows[1][index]
+        to_first = lax.ppermute(first_one, "section", [(1, 0)])
+        to_second = lax.ppermute(second_one, "section", [(0, 1)])
+        mine = per_core(core, first_one, second_one)
+        theirs = per_core(core, to_first, to_second)
         return jnp.concatenate([mine, theirs], axis=0)
 
     arrived_all, hidden_grad_all, active_all, rows_grad_all = [joined_rows(i) for i in range(4)]

time: 361 us -> 360 us (level)
  Pallas kernels: 205 us -> 193 us
  matrix products: 69.9 us -> 61.9 us
  local copies, waits for them, and re-layouts: 30.1 us -> 37.4 us
  starting transfers between devices: 30 us -> 36 us
  other arithmetic: 21.7 us -> 25.4 us
    ppermute x0 -> x8, starting transfers between devices: none -> 32.6 us  [the longest x4 26.8 us: joined_rows(): to_first = lax.ppermute(first_one, 'section', [(1, 0)])]
    ppermute x11 -> x7, starting transfers between devices: 30 us -> 3.41 us  [swap_cores(): return lax.ppermute(block, 'section', [(0, 1), (1, 0)])]
    pallas_call x5 -> x4, Pallas kernels: 111 us -> 105 us  [spread(): pl.pallas_call(lambda *refs: spread_kernel(groups, both, *refs), out_shap...]
    unnamed x194 -> x218, local copies, waits for them, and re-layouts: 7.35 us -> 13.4 us
    pallas_call x5 -> x4, Pallas kernels: 94 us -> 88.8 us  [collapse(): pl.pallas_call(lambda *refs: collapse_kernel(groups, total, *refs), out_s...]
    select_n x8 -> x11, other arithmetic: 5.4 us -> 8.62 us  [per_core(): return jnp.where(section_index == 0, first_one, second_one)]
  transfers between devices with their start and end apart: 11 -> 15, of which waited for: 0 -> 2; matrix products, arithmetic and copies ran while one was open for 16% -> 31% of each run, Pallas kernels for 21% -> 39%
where the time goes in v3:
time: 360 us; the launch traced here: 358 us
  Pallas kernels  193 us (54%)
  matrix products  61.9 us (17%)
  local copies, waits for them, and re-layouts  37.4 us (10%)
  starting transfers between devices  36 us (10%)
  other arithmetic  25.4 us (7%)
    pallas_call x4, Pallas kernels, spread(): pl.pallas_call(lambda *refs: spread_kernel(groups, both, *refs), out_shap...  105 us
    pallas_call x4, Pallas kernels, collapse(): pl.pallas_call(lambda *refs: collapse_kernel(groups, total, *refs), out_s...  88.8 us
    ppermute x4, starting transfers between devices, joined_rows(): to_first = lax.ppermute(first_one, 'section', [(1, 0)])  26.8 us
    unnamed x218, local copies, waits for them, and re-layouts  13.4 us
    select_n x11, other arithmetic, per_core(): return jnp.where(section_index == 0, first_one, second_one)  8.62 us
  transfers between devices with their start and end apart: 15, of which 2 were waited for; matrix products, arithmetic and copies ran while one was open for 31% of the time, Pallas kernels for 39%

profile of v3, /device:TPU:13, one launch (start us, length us, event | category | flops | bytes accessed | tf_op | source)
XLA Modules:
  0.0 357.7 jit_solution(5819306428203394199)
XLA Ops:
  8.6 51.1 %shard_map.204 = bf16[2,16,48,3328]{3,2,1,0:T(8,128)(2,1)} custom-call(bf16[48,3328]{1,0:T(8,128)(2,1)} %fusion.63.refs_0_), custom_call_target="tpu_custom_call" | custom-call | tf_op jit(solution)/shard_map/pallas_call | solution.py:205
  59.7 7.0 %fusion.204 = (bf16[1,16,48,3328]{3,2,1,0:T(8,128)(2,1)}, bf16[1,16,48,3328]{3,2,1,0:T(8,128)(2,1)S(1)}) fusion(bf16[2,16,48,3328]{3,2,1,0:T(8,128)(2,1)} %shard_map.204), kind=kLoop, calls=%fused_computation.370 | loop fusion | bytes 20447232 | tf_op jit(solution)/shard_map/slice | solution.py:609
  66.7 2.3 copy-done
  71.0 2.9 convolution_convert_fusion.2
  80.7 1.8 multiply_reduce_fusion.7
  88.6 23.3 %shard_map.205 = bf16[16,24,768]{2,1,0:T(8,128)(2,1)} custom-call(bf16[4,24,768]{2,1,0:T(8,128)(2,1)} %convolution_convert_fusion.15.refs_0_), custom_call_target="tpu_custom_call" | custom-call | tf_op jit(solution)/shard_map/pallas_call | solution.py:205
  112.0 5.7 %collective-permute-start.7 = (bf16[384,768]{1,0:T(8,128)(2,1)}, bf16[384,768]{1,0:T(8,128)(2,1)}, u32[]{:S(2)}, u32[]{:S(2)}) collective-permute-start(bf16[384,768]{1,0:T(8,128)(2,1)} %bitcast.237), channel_id=1, source_target_pairs={{16,0},{17,1},{18,2},{19,3},{20,4},{21,5},{22,6},{23,7},{24,8},{25... | collective-permute-start | bytes 1769480 | tf_op jit(solution)/shard_map/ppermute | solution.py:692
  118.1 3.7 %multiply_convert_fusion.1 = (bf16[384,768]{1,0:T(8,128)(2,1)S(1)}, f32[384,768]{1,0:T(8,128)}) fusion(bf16[384,768]{1,0:T(8,128)(2,1)} %bitcast.238, bf16[768,768]{1,0:T(8,128)(2,1)} %collective-permute-done.1, pred[]{:T(512)S(6)} %eq.70, bf16[1,1,768,768]{3,2,1,0:T(8,128)(2,1)} %param.23), kind=kOutput, calls=%fused_computation.73 | convolution fusion | flops 456228864 | bytes 4718593 | tf_op jit(solution)/shard_map/dot_general | solution.py:385
  121.9 2.1 convolution_convert_fusion.7
  124.1 11.0 %shard_map.206 = bf16[4,24,768]{2,1,0:T(8,128)(2,1)S(1)} custom-call(bf16[16,24,768]{2,1,0:T(8,128)(2,1)S(1)} %bitcast.218), custom_call_target="tpu_custom_call" | custom-call | tf_op jit(solution)/shard_map/pallas_call | solution.py:296
  138.7 1.8 multiply_reduce_fusion.6
  143.6 17.8 %shard_map.207 = bf16[16,48,768]{2,1,0:T(8,128)(2,1)} custom-call(bf16[4,48,768]{2,1,0:T(8,128)(2,1)} %pad_maximum_fusion.2.refs_0_), custom_call_target="tpu_custom_call" | custom-call | tf_op jit(solution)/shard_map/pallas_call | solution.py:205
  161.4 2.3 fusion.207
  163.7 1.8 broadcast_select_fusion.9
  166.3 2.3 fusion.29
  169.5 12.6 %shard_map.208 = bf16[4,48,768]{2,1,0:T(8,128)(2,1)S(1)} custom-call(bf16[16,48,768]{2,1,0:T(8,128)(2,1)S(1)} %pad_maximum_fusion.1.refs_0_), custom_call_target="tpu_custom_call" | custom-call | tf_op jit(solution)/shard_map/pallas_call | solution.py:296
  185.2 1.8 convolution_convert_fusion.17
  194.3 3.4 fusion.100
  198.9 12.4 %shard_map.209 = bf16[16,24,768]{2,1,0:T(8,128)(2,1)} custom-call(bf16[4,24,768]{2,1,0:T(8,128)(2,1)} %convolution_convert_fusion.12.refs_0_), custom_call_target="tpu_custom_call" | custom-call | tf_op jit(solution)/shard_map/pallas_call | solution.py:205
  211.3 2.6 broadcast_select_fusion.7
  213.9 17.5 %collective-permute-start.13 = (bf16[384,768]{1,0:T(8,128)(2,1)S(1)}, bf16[384,768]{1,0:T(8,128)(2,1)}, u32[]{:S(2)}, u32[]{:S(2)}) collective-permute-start(bf16[384,768]{1,0:T(8,128)(2,1)S(1)} %bitcast.239), channel_id=1, source_target_pairs={{16,0},{17,1},{18,2},{19,3},{20,4},{21,5},{22,6},{23,7},{24,8},{25... | collective-permute-start | bytes 1769480 | tf_op jit(solution)/shard_map/ppermute | solution.py:692
  231.4 3.5 broadcast_select_fusion.11
  234.9 2.2 convolution_convert_fusion.4
  237.1 10.4 %shard_map.210 = bf16[4,24,768]{2,1,0:T(8,128)(2,1)S(1)} custom-call(bf16[16,24,768]{2,1,0:T(8,128)(2,1)S(1)} %bitcast.217), custom_call_target="tpu_custom_call" | custom-call | tf_op jit(solution)/shard_map/pallas_call | solution.py:296
  249.4 1.8 convolution_convert_fusion.16
  254.6 2.2 convolution_convert_fusion.8
  262.0 3.4 fusion.103
  274.1 2.3 broadcast_select_fusion.4
  279.5 2.3 collective-permute-start.11
  290.6 2.5 convolution_bitcast_fusion
  294.4 2.5 convolution_bitcast_fusion.1
  299.4 54.7 %shard_map.211 = f32[48,3328]{1,0:T(8,128)S(1)} custom-call(bf16[16,48,3328]{2,1,0:T(8,128)(2,1)S(1)} %pad_maximum_fusion.refs_0_), custom_call_target="tpu_custom_call" | custom-call | tf_op jit(solution)/shard_map/pallas_call | solution.py:296
  (395 shorter events, 80.2 us)
Async XLA Ops:
  1.8 85.7 %collective-permute-start = (s32[64]{0:T(128)}, s32[64]{0:T(128)S(1)}, u32[]{:S(2)}, u32[]{:S(2)}) collective-permute-start(s32[64]{0:T(128)} %fusion.185), channel_id=1, source_target_pairs={{0,16},{16,0},{1,17},{17,1},{2,18},{18,2},{3,19},{19,3},{4,20},{20... | collective-permute-start | bytes 776 | tf_op jit(solution)/shard_map/ppermute | solution.py:550
  2.5 115.6 %collective-permute-start.1 = (bf16[768,768]{1,0:T(8,128)(2,1)}, bf16[768,768]{1,0:T(8,128)(2,1)}, u32[]{:S(2)}, u32[]{:S(2)}) collective-permute-start(bf16[768,768]{1,0:T(8,128)(2,1)} %bitcast.275), channel_id=1, source_target_pairs={{0,16},{16,0},{1,17},{17,1},{2,18},{18,2},{3,19},{19,3},{4,20},{20... | collective-permute-start | bytes 3538952 | tf_op jit(solution)/shard_map/ppermute | solution.py:550
  2.5 119.4 %collective-permute-start.2 = (bf16[768,768]{1,0:T(8,128)(2,1)}, bf16[768,768]{1,0:T(8,128)(2,1)}, u32[]{:S(2)}, u32[]{:S(2)}) collective-permute-start(bf16[768,768]{1,0:T(8,128)(2,1)} %bitcast.274), channel_id=1, source_target_pairs={{0,16},{16,0},{1,17},{17,1},{2,18},{18,2},{3,19},{19,3},{4,20},{20... | collective-permute-start | bytes 3538952 | tf_op jit(solution)/shard_map/ppermute | solution.py:550
  5.4 68.5 %copy-start.79 = (f32[64]{0:T(128)}, f32[64]{0:T(128)S(1)}, u32[]{:S(2)}) copy-start(f32[64]{0:T(128)S(1)} %add_rsqrt_fusion.3) | copy-start | bytes 772
  84.0 33.9 %copy-start.44 = (f32[64]{0:T(128)}, f32[64]{0:T(128)S(1)}, u32[]{:S(2)}) copy-start(f32[64]{0:T(128)S(1)} %get-tuple-element.105) | copy-start | bytes 772
  86.5 35.4 %copy-start.57 = (f32[64]{0:T(128)}, f32[64]{0:T(128)S(1)}, u32[]{:S(2)}) copy-start(f32[64]{0:T(128)S(1)} %fusion.156) | copy-start | bytes 772
  87.5 34.4 %copy-start.67 = (s32[64]{0:T(128)}, s32[64]{0:T(128)S(1)}, u32[]{:S(2)}) copy-start(s32[64]{0:T(128)S(1)} %get-tuple-element.98) | copy-start | bytes 772
  87.5 54.6 %copy-start.64 = (s32[64]{0:T(128)}, s32[64]{0:T(128)S(1)}, u32[]{:S(2)}) copy-start(s32[64]{0:T(128)S(1)} %get-tuple-element.97) | copy-start | bytes 772
  87.7 47.3 %copy-start.62 = (s32[64]{0:T(128)}, s32[64]{0:T(128)S(1)}, u32[]{:S(2)}) copy-start(s32[64]{0:T(128)S(1)} %multiply_add_fusion.2) | copy-start | bytes 772
  88.6 47.5 %slice-start = ((s8[5111808]{0:T(1024)(128)(4,1)}), s8[917504]{0:T(1024)(128)(4,1)S(1)}, s32[]{:S(2)}) async-start(s8[5111808]{0:T(1024)(128)(4,1)} %bitcast.233), calls=%async_computation | async-start | bytes 1835008
  112.0 181.2 %collective-permute-start.7 = (bf16[384,768]{1,0:T(8,128)(2,1)}, bf16[384,768]{1,0:T(8,128)(2,1)}, u32[]{:S(2)}, u32[]{:S(2)}) collective-permute-start(bf16[384,768]{1,0:T(8,128)(2,1)} %bitcast.237), channel_id=1, source_target_pairs={{16,0},{17,1},{18,2},{19,3},{20,4},{21,5},{22,6},{23,7},{24,8},{25... | collective-permute-start | bytes 1769480 | tf_op jit(solution)/shard_map/ppermute | solution.py:692
  136.2 46.0 %copy-start.77 = (f32[64]{0:T(128)}, f32[64]{0:T(128)S(1)}, u32[]{:S(2)}) copy-start(f32[64]{0:T(128)S(1)} %add_rsqrt_fusion.1) | copy-start | bytes 772
  140.5 44.5 %copy-start.70 = (f32[64]{0:T(128)}, f32[64]{0:T(128)S(1)}, u32[]{:S(2)}) copy-start(f32[64]{0:T(128)S(1)} %add_rsqrt_fusion) | copy-start | bytes 772
  141.8 41.8 %copy-start.47 = (f32[64]{0:T(128)}, f32[64]{0:T(128)S(1)}, u32[]{:S(2)}) copy-start(f32[64]{0:T(128)S(1)} %get-tuple-element.112) | copy-start | bytes 772
  142.2 41.5 %copy-start.60 = (f32[64]{0:T(128)}, f32[64]{0:T(128)S(1)}, u32[]{:S(2)}) copy-start(f32[64]{0:T(128)S(1)} %fusion.158) | copy-start | bytes 772
  142.4 41.3 %copy-start.52 = (f32[64]{0:T(128)}, f32[64]{0:T(128)S(1)}, u32[]{:S(2)}) copy-start(f32[64]{0:T(128)S(1)} %select_reduce_fusion) | copy-start | bytes 772
  185.0 88.9 %copy-start.37 = (f32[768]{0:T(1024)}, f32[768]{0:T(1024)S(1)}, u32[]{:S(2)}) copy-start(f32[768]{0:T(1024)S(1)} %get-tuple-element.54) | copy-start | bytes 9220
  190.2 93.8 %collective-permute-start.14 = (bf16[384,768]{1,0:T(8,128)(2,1)}, bf16[384,768]{1,0:T(8,128)(2,1)}, u32[]{:S(2)}, u32[]{:S(2)}) collective-permute-start(bf16[384,768]{1,0:T(8,128)(2,1)} %bitcast.31), channel_id=1, source_target_pairs={{0,16},{1,17},{2,18},{3,19},{4,20},{5,21},{6,22},{7,23},{8,24},{9,... | collective-permute-start | bytes 1769480 | tf_op jit(solution)/shard_map/ppermute | solution.py:693
  191.5 94.9 %collective-permute-start.12 = (bf16[384,768]{1,0:T(8,128)(2,1)}, bf16[384,768]{1,0:T(8,128)(2,1)}, u32[]{:S(2)}, u32[]{:S(2)}) collective-permute-start(bf16[384,768]{1,0:T(8,128)(2,1)} %copy-done.94), channel_id=1, source_target_pairs={{0,16},{1,17},{2,18},{3,19},{4,20},{5,21},{6,22},{7,23},{8,24},{9,... | collective-permute-start | bytes 1769480 | tf_op jit(solution)/shard_map/ppermute | solution.py:693
  197.7 76.2 %copy-start.42 = (f32[768]{0:T(1024)}, f32[768]{0:T(1024)S(1)}, u32[]{:S(2)}) copy-start(f32[768]{0:T(1024)S(1)} %get-tuple-element.58) | copy-start | bytes 9220
  198.0 49.9 %copy-start.74 = (f32[64]{0:T(128)}, f32[64]{0:T(128)S(1)}, u32[]{:S(2)}) copy-start(f32[64]{0:T(128)S(1)} %get-tuple-element.64) | copy-start | bytes 772
  211.3 20.1 %copy-start.86 = (bf16[1,1,768,768]{3,2,1,0:T(8,128)(2,1)S(1)}, bf16[1,1,768,768]{3,2,1,0:T(8,128)(2,1)}, u32[]{:S(2)}) copy-start(bf16[1,1,768,768]{3,2,1,0:T(8,128)(2,1)} %param.24) | copy-start | bytes 3538948
  211.3 20.1 %copy-start.92 = (bf16[384,768]{1,0:T(8,128)(2,1)S(1)}, bf16[384,768]{1,0:T(8,128)(2,1)}, u32[]{:S(2)}) copy-start(bf16[384,768]{1,0:T(8,128)(2,1)} %copy-done.91) | copy-start | bytes 1769476
  213.9 68.7 %collective-permute-start.13 = (bf16[384,768]{1,0:T(8,128)(2,1)S(1)}, bf16[384,768]{1,0:T(8,128)(2,1)}, u32[]{:S(2)}, u32[]{:S(2)}) collective-permute-start(bf16[384,768]{1,0:T(8,128)(2,1)S(1)} %bitcast.239), channel_id=1, source_target_pairs={{16,0},{17,1},{18,2},{19,3},{20,4},{21,5},{22,6},{23,7},{24,8},{25... | collective-permute-start | bytes 1769480 | tf_op jit(solution)/shard_map/ppermute | solution.py:692
  274.0 2.6 collective-permute-start.6
  276.6 1.5 collective-permute-start.3
  278.0 1.4 collective-permute-start.4
  279.5 8.6 %collective-permute-start.11 = (bf16[384,768]{1,0:T(8,128)(2,1)}, bf16[384,768]{1,0:T(8,128)(2,1)S(1)}, u32[]{:S(2)}, u32[]{:S(2)}) collective-permute-start(bf16[384,768]{1,0:T(8,128)(2,1)} %copy-done.89), channel_id=1, source_target_pairs={{16,0},{17,1},{18,2},{19,3},{20,4},{21,5},{22,6},{23,7},{24,8},{25... | collective-permute-start | bytes 1769480 | tf_op jit(solution)/shard_map/ppermute | solution.py:692
  282.6 10.5 %collective-permute-start.9 = (bf16[384,768]{1,0:T(8,128)(2,1)S(1)}, bf16[384,768]{1,0:T(8,128)(2,1)S(1)}, u32[]{:S(2)}, u32[]{:S(2)}) collective-permute-start(bf16[384,768]{1,0:T(8,128)(2,1)S(1)} %copy-done.96), channel_id=1, source_target_pairs={{16,0},{17,1},{18,2},{19,3},{20,4},{21,5},{22,6},{23,7},{24,8},{25... | collective-permute-start | bytes 1769480 | tf_op jit(solution)/shard_map/ppermute | solution.py:692
  284.0 9.1 %collective-permute-start.10 = (bf16[384,768]{1,0:T(8,128)(2,1)S(1)}, bf16[384,768]{1,0:T(8,128)(2,1)S(1)}, u32[]{:S(2)}, u32[]{:S(2)}) collective-permute-start(bf16[384,768]{1,0:T(8,128)(2,1)S(1)} %copy-done.93), channel_id=1, source_target_pairs={{0,16},{1,17},{2,18},{3,19},{4,20},{5,21},{6,22},{7,23},{8,24},{9,... | collective-permute-start | bytes 1769480 | tf_op jit(solution)/shard_map/ppermute | solution.py:693
  286.4 6.8 %collective-permute-start.8 = (bf16[384,768]{1,0:T(8,128)(2,1)S(1)}, bf16[384,768]{1,0:T(8,128)(2,1)S(1)}, u32[]{:S(2)}, u32[]{:S(2)}) collective-permute-start(bf16[384,768]{1,0:T(8,128)(2,1)S(1)} %bitcast.242), channel_id=1, source_target_pairs={{0,16},{1,17},{2,18},{3,19},{4,20},{5,21},{6,22},{7,23},{8,24},{9,... | collective-permute-start | bytes 1769480 | tf_op jit(solution)/shard_map/ppermute | solution.py:693
  288.2 8.8 %collective-permute-start.5 = (bf16[64,5380]{1,0:T(8,128)(2,1)S(1)}, bf16[64,5380]{1,0:T(8,128)(2,1)S(1)}, u32[]{:S(2)}, u32[]{:S(2)}) collective-permute-start(bf16[64,5380]{1,0:T(8,128)(2,1)S(1)} %copy-done.16), channel_id=1, source_target_pairs={{0,16},{16,0},{1,17},{17,1},{2,18},{18,2},{3,19},{19,3},{4,20},{20... | collective-permute-start | bytes 2065928 | tf_op jit(solution)/shard_map/ppermute | solution.py:550
  (85 other events, 388.0 us)

commit v4 on v3

--- a/solution.py
+++ b/solution.py
@@ -688,11 +688,8 @@
     total = collapse(packed.reshape(dp_count, -1, packed.shape[1]), True, 3)
 
     def joined_rows(index):
-        first_one, second_one = expert_rows[0][index], expert_rows[1][index]
-        to_first = lax.ppermute(first_one, "section", [(1, 0)])
-        to_second = lax.ppermute(second_one, "section", [(0, 1)])
-        mine = per_core(core, first_one, second_one)
-        theirs = per_core(core, to_first, to_second)
+        mine = per_core(core, expert_rows[0][index], expert_rows[1][index])
+        theirs = swap_cores(per_core(core, expert_rows[1][index], expert_rows[0][index]))
         return jnp.concatenate([mine, theirs], axis=0)
 
     arrived_all, hidden_grad_all, active_all, rows_grad_all = [joined_rows(i) for i in range(4)]

time: 360 us -> 334 us (0.928)
  starting transfers between devices: 36 us -> 23.4 us
  local copies, waits for them, and re-layouts: 37.4 us -> 29.5 us
  other arithmetic: 25.4 us -> 20.6 us
  Pallas kernels: 193 us -> 189 us
  matrix products: 61.9 us -> 65.7 us
    ppermute x8 -> x0, starting transfers between devices: 32.6 us -> none  [the longest x4 26.8 us: joined_rows(): to_first = lax.ppermute(first_one, 'section', [(1, 0)])]
    ppermute x7 -> x11, starting transfers between devices: 3.41 us -> 23.4 us  [swap_cores(): return lax.ppermute(block, 'section', [(0, 1), (1, 0)])]
    unnamed x218 -> x228, local copies, waits for them, and re-layouts: 13.4 us -> 6.67 us
    select_n x11 -> x8, other arithmetic: 8.62 us -> 6.52 us  [per_core(): return jnp.where(section_index == 0, first_one, second_one)]
  transfers between devices with their start and end apart: 15 -> 11, of which waited for: 2 -> 2; matrix products, arithmetic and copies ran while one was open for 31% -> 15% of each run, Pallas kernels for 39% -> 22%
where the time goes in v4:
time: 334 us; the launch traced here: 332 us
  Pallas kernels  189 us (57%)
  matrix products  65.7 us (20%)
  local copies, waits for them, and re-layouts  29.5 us (9%)
  starting transfers between devices  23.4 us (7%)
  other arithmetic  20.6 us (6%)
    pallas_call x4, Pallas kernels, spread(): pl.pallas_call(lambda *refs: spread_kernel(groups, both, *refs), out_shap...  101 us
    pallas_call x4, Pallas kernels, collapse(): pl.pallas_call(lambda *refs: collapse_kernel(groups, total, *refs), out_s...  87.4 us
    ppermute x11, starting transfers between devices, swap_cores(): return lax.ppermute(block, 'section', [(0, 1), (1, 0)])  23.4 us
    dot_general x2, matrix products, layer_backward(): jnp.einsum('te,de->td', qkv_grad, w_qkv, preferred_element_type=jnp.float32)  7.96 us
    slice x1, local copies, waits for them, and re-layouts, shards(): packs[layer].reshape(width, own_pack.shape[1])  6.99 us
  transfers between devices with their start and end apart: 11, of which 2 were waited for; matrix products, arithmetic and copies ran while one was open for 15% of the time, Pallas kernels for 22%

profile of v4, /device:TPU:13, one launch (start us, length us, event | category | flops | bytes accessed | tf_op | source)
XLA Modules:
  0.0 332.3 jit_solution(13022626574311589802)
XLA Ops:
  3.6 1.7 fusion.101
  6.9 1.7 fusion.63.refs_0_
  8.6 51.1 %shard_map.204 = bf16[2,16,48,3328]{3,2,1,0:T(8,128)(2,1)} custom-call(bf16[48,3328]{1,0:T(8,128)(2,1)} %fusion.63.refs_0_), custom_call_target="tpu_custom_call" | custom-call | tf_op jit(solution)/shard_map/pallas_call | solution.py:205
  59.7 7.0 %fusion.204 = (bf16[1,16,48,3328]{3,2,1,0:T(8,128)(2,1)}, bf16[1,16,48,3328]{3,2,1,0:T(8,128)(2,1)S(1)}) fusion(bf16[2,16,48,3328]{3,2,1,0:T(8,128)(2,1)} %shard_map.204), kind=kLoop, calls=%fused_computation.370 | loop fusion | bytes 20447232 | tf_op jit(solution)/shard_map/slice | solution.py:609
  66.7 2.3 copy-done
  71.0 2.9 convolution_convert_fusion.2
  79.4 1.8 multiply_reduce_fusion.7
  82.8 1.6 fusion.205
  88.4 23.3 %shard_map.205 = bf16[16,24,768]{2,1,0:T(8,128)(2,1)} custom-call(bf16[4,24,768]{2,1,0:T(8,128)(2,1)} %convolution_convert_fusion.15.refs_0_), custom_call_target="tpu_custom_call" | custom-call | tf_op jit(solution)/shard_map/pallas_call | solution.py:205
  111.9 2.6 fusion.59
  114.6 2.9 convolution_convert_fusion.7
  117.5 9.7 %shard_map.206 = bf16[4,24,768]{2,1,0:T(8,128)(2,1)S(1)} custom-call(bf16[16,24,768]{2,1,0:T(8,128)(2,1)S(1)} %bitcast.218), custom_call_target="tpu_custom_call" | custom-call | tf_op jit(solution)/shard_map/pallas_call | solution.py:296
  131.2 1.8 multiply_reduce_fusion.6
  136.1 16.1 %shard_map.207 = bf16[16,48,768]{2,1,0:T(8,128)(2,1)} custom-call(bf16[4,48,768]{2,1,0:T(8,128)(2,1)} %pad_maximum_fusion.2.refs_0_), custom_call_target="tpu_custom_call" | custom-call | tf_op jit(solution)/shard_map/pallas_call | solution.py:205
  154.2 2.3 broadcast_select_fusion.9
  159.7 12.3 %shard_map.208 = bf16[4,48,768]{2,1,0:T(8,128)(2,1)S(1)} custom-call(bf16[16,48,768]{2,1,0:T(8,128)(2,1)S(1)} %pad_maximum_fusion.1.refs_0_), custom_call_target="tpu_custom_call" | custom-call | tf_op jit(solution)/shard_map/pallas_call | solution.py:296
  173.5 1.8 multiply_reduce_fusion.2
  175.5 1.8 convolution_convert_fusion.17
  180.7 2.1 convolution_convert_fusion.9
  185.9 3.9 %fusion.100 = (f32[768]{0:T(1024)}, f32[64]{0:T(128)S(1)}, f32[64,768]{1,0:T(8,128)S(1)}) fusion(bf16[64,768]{1,0:T(8,128)(2,1)S(1)} %get-tuple-element.67, f32[64]{0:T(128)S(1)} %copy-done.95, f32[768]{0:T(1024)S(1)} %convert_reduce_fusion.4, bf16[768,3328]{1,0:T(8,128)(2,1)} %bitcast.232, bf16[64,768]{1,0:T(8,128)(2,1)S(1)} %copy.266, ...), kind=kOutput, calls=%fused_computation.187 | convolution fusion | flops 227769536 | bytes 4135424 | tf_op jit(solution)/shard_map/te,de->td/dot_general | solution.py:516
  190.9 11.0 %shard_map.209 = bf16[16,24,768]{2,1,0:T(8,128)(2,1)} custom-call(bf16[4,24,768]{2,1,0:T(8,128)(2,1)} %convolution_convert_fusion.12.refs_0_), custom_call_target="tpu_custom_call" | custom-call | tf_op jit(solution)/shard_map/pallas_call | solution.py:205
  202.0 2.3 broadcast_select_fusion.7
  204.3 4.2 %broadcast_select_fusion.11 = (bf16[384,768]{1,0:T(8,128)(2,1)}, bf16[384,768]{1,0:T(8,128)(2,1)}, bf16[384,768]{1,0:T(8,128)(2,1)S(1)}) fusion(bf16[384,768]{1,0:T(8,128)(2,1)S(1)} %copy-done.102, pred[]{:T(512)S(6)} %eq.70, f32[384,768]{1,0:T(8,128)S(1)} %copy-done.12, bf16[384,768]{1,0:T(8,128)(2,1)S(1)} %bitcast.238, ...), kind=kOutput, calls=%fused_computation.122 | convolution fusion | flops 460062720 | bytes 6488065 | tf_op jit(solution)/shard_map/rd,fd->rf/dot_general | solution.py:334
  208.6 2.0 convolution_convert_fusion.4
  210.5 11.6 %shard_map.210 = bf16[4,24,768]{2,1,0:T(8,128)(2,1)S(1)} custom-call(bf16[16,24,768]{2,1,0:T(8,128)(2,1)S(1)} %bitcast.217), custom_call_target="tpu_custom_call" | custom-call | tf_op jit(solution)/shard_map/pallas_call | solution.py:296
  222.5 1.8 multiply_reduce_fusion.3
  225.2 1.8 convolution_convert_fusion.16
  231.4 20.7 %collective-permute-start.10 = (bf16[384,768]{1,0:T(8,128)(2,1)}, bf16[384,768]{1,0:T(8,128)(2,1)}, u32[]{:S(2)}, u32[]{:S(2)}) collective-permute-start(bf16[384,768]{1,0:T(8,128)(2,1)} %get-tuple-element.83), channel_id=1, source_target_pairs={{0,16},{16,0},{1,17},{17,1},{2,18},{18,2},{3,19},{19,3},{4,20},{20... | collective-permute-start | bytes 1769480 | tf_op jit(solution)/shard_map/ppermute | solution.py:550
  253.7 4.1 %fusion.103 = (f32[768]{0:T(1024)S(1)}, f32[64]{0:T(128)S(1)}, f32[64,768]{1,0:T(8,128)}) fusion(bf16[1,64,768]{2,1,0:T(8,128)(2,1)S(1)} %copy-done.3, f32[64]{0:T(128)S(1)} %copy-done.97, f32[768]{0:T(1024)S(1)} %copy-done.48, bf16[768,3328]{1,0:T(8,128)(2,1)} %bitcast.226, bf16[64,768]{1,0:T(8,128)(2,1)S(1)} %copy.267, ...), kind=kOutput, calls=%fused_computation.190 | convolution fusion | flops 227769536 | bytes 4135424 | tf_op jit(solution)/shard_map/te,de->td/dot_general | solution.py:516
  264.8 3.9 %convolution_bitcast_fusion = f32[1,1,768,768]{3,2,1,0:T(8,128)} fusion(bf16[384,768]{1,0:T(8,128)(2,1)} %collective-permute-done.9, bf16[384,768]{1,0:T(8,128)(2,1)S(1)} %copy-done.103, bf16[384,768]{1,0:T(8,128)(2,1)} %collective-permute-done.10, bf16[384,768]{1,0:T(8,128)(2,1)S(1)} %copy-done.24), kind=kOutput, calls=%fused_computation.24 | convolution fusion | flops 910688256 | bytes 4718592 | tf_op jit(solution)/shard_map/rf,rd->fd/dot_general | solution.py:699
  268.7 3.8 %convolution_bitcast_fusion.1 = f32[1,1,768,768]{3,2,1,0:T(8,128)} fusion(bf16[384,768]{1,0:T(8,128)(2,1)} %collective-permute-done.7, bf16[384,768]{1,0:T(8,128)(2,1)S(1)} %copy-done.23, bf16[384,768]{1,0:T(8,128)(2,1)} %collective-permute-done.8, bf16[384,768]{1,0:T(8,128)(2,1)S(1)} %copy-done.104), kind=kOutput, calls=%fused_computation.25 | convolution fusion | flops 910688256 | bytes 4718592 | tf_op jit(solution)/shard_map/rd,rf->df/dot_general | solution.py:696
  274.9 53.8 %shard_map.211 = f32[48,3328]{1,0:T(8,128)S(1)} custom-call(bf16[16,48,3328]{2,1,0:T(8,128)(2,1)S(1)} %pad_maximum_fusion.refs_0_), custom_call_target="tpu_custom_call" | custom-call | tf_op jit(solution)/shard_map/pallas_call | solution.py:296
  (393 shorter events, 58.0 us)
Async XLA Ops:
  1.8 84.6 %collective-permute-start = (s32[64]{0:T(128)}, s32[64]{0:T(128)}, u32[]{:S(2)}, u32[]{:S(2)}) collective-permute-start(s32[64]{0:T(128)} %fusion.185), channel_id=1, source_target_pairs={{0,16},{16,0},{1,17},{17,1},{2,18},{18,2},{3,19},{19,3},{4,20},{20... | collective-permute-start | bytes 776 | tf_op jit(solution)/shard_map/ppermute | solution.py:550
  2.5 109.4 %collective-permute-start.1 = (bf16[768,768]{1,0:T(8,128)(2,1)}, bf16[768,768]{1,0:T(8,128)(2,1)}, u32[]{:S(2)}, u32[]{:S(2)}) collective-permute-start(bf16[768,768]{1,0:T(8,128)(2,1)} %bitcast.250), channel_id=1, source_target_pairs={{0,16},{16,0},{1,17},{17,1},{2,18},{18,2},{3,19},{19,3},{4,20},{20... | collective-permute-start | bytes 3538952 | tf_op jit(solution)/shard_map/ppermute | solution.py:550
  2.5 112.0 %collective-permute-start.2 = (bf16[768,768]{1,0:T(8,128)(2,1)}, bf16[768,768]{1,0:T(8,128)(2,1)}, u32[]{:S(2)}, u32[]{:S(2)}) collective-permute-start(bf16[768,768]{1,0:T(8,128)(2,1)} %bitcast.273), channel_id=1, source_target_pairs={{0,16},{16,0},{1,17},{17,1},{2,18},{18,2},{3,19},{19,3},{4,20},{20... | collective-permute-start | bytes 3538952 | tf_op jit(solution)/shard_map/ppermute | solution.py:550
  5.4 68.5 %copy-start.96 = (f32[64]{0:T(128)}, f32[64]{0:T(128)S(1)}, u32[]{:S(2)}) copy-start(f32[64]{0:T(128)S(1)} %add_rsqrt_fusion.3) | copy-start | bytes 772
  81.4 141.0 %copy-start.42 = (f32[768]{0:T(1024)}, f32[768]{0:T(1024)S(1)}, u32[]{:S(2)}) copy-start(f32[768]{0:T(1024)S(1)} %convert_reduce_fusion.5) | copy-start | bytes 9220
  82.7 29.0 %copy-start.56 = (f32[64]{0:T(128)}, f32[64]{0:T(128)S(1)}, u32[]{:S(2)}) copy-start(f32[64]{0:T(128)S(1)} %get-tuple-element.109) | copy-start | bytes 772
  85.4 29.2 %copy-start.80 = (f32[64]{0:T(128)}, f32[64]{0:T(128)S(1)}, u32[]{:S(2)}) copy-start(f32[64]{0:T(128)S(1)} %fusion.156) | copy-start | bytes 772
  85.4 90.0 %copy-start.44 = (f32[768]{0:T(1024)}, f32[768]{0:T(1024)S(1)}, u32[]{:S(2)}) copy-start(f32[768]{0:T(1024)S(1)} %convert_reduce_fusion.3) | copy-start | bytes 9220
  87.1 27.4 %copy-start.67 = (s32[64]{0:T(128)}, s32[64]{0:T(128)S(1)}, u32[]{:S(2)}) copy-start(s32[64]{0:T(128)S(1)} %get-tuple-element.104) | copy-start | bytes 772
  87.1 47.8 %copy-start.64 = (s32[64]{0:T(128)}, s32[64]{0:T(128)S(1)}, u32[]{:S(2)}) copy-start(s32[64]{0:T(128)S(1)} %get-tuple-element.103) | copy-start | bytes 772
  87.5 39.7 %copy-start.62 = (s32[64]{0:T(128)}, s32[64]{0:T(128)S(1)}, u32[]{:S(2)}) copy-start(s32[64]{0:T(128)S(1)} %get-tuple-element.130) | copy-start | bytes 772
  87.5 47.7 %copy-start.73 = (s32[64]{0:T(128)}, s32[64]{0:T(128)S(1)}, u32[]{:S(2)}) copy-start(s32[64]{0:T(128)S(1)} %get-tuple-element.129) | copy-start | bytes 772
  111.9 15.4 %copy-start.70 = (f32[64]{0:T(128)}, f32[64]{0:T(128)S(1)}, u32[]{:S(2)}) copy-start(f32[64]{0:T(128)S(1)} %select_reduce_fusion.1) | copy-start | bytes 772
  111.9 16.4 %slice-start = ((s8[5111808]{0:T(1024)(128)(4,1)}), s8[4194304]{0:T(1024)(128)(4,1)S(1)}, s32[]{:S(2)}) async-start(s8[5111808]{0:T(1024)(128)(4,1)} %bitcast.233), calls=%async_computation | async-start | bytes 8388608
  134.3 17.9 %copy-start.59 = (f32[64]{0:T(128)}, f32[64]{0:T(128)S(1)}, u32[]{:S(2)}) copy-start(f32[64]{0:T(128)S(1)} %get-tuple-element.116) | copy-start | bytes 772
  134.9 38.5 %copy-start.83 = (f32[64]{0:T(128)}, f32[64]{0:T(128)S(1)}, u32[]{:S(2)}) copy-start(f32[64]{0:T(128)S(1)} %fusion.158) | copy-start | bytes 772
  135.2 38.3 %copy-start.75 = (f32[64]{0:T(128)}, f32[64]{0:T(128)S(1)}, u32[]{:S(2)}) copy-start(f32[64]{0:T(128)S(1)} %select_reduce_fusion) | copy-start | bytes 772
  190.0 32.4 %copy-start.90 = (f32[64]{0:T(128)}, f32[64]{0:T(128)S(1)}, u32[]{:S(2)}) copy-start(f32[64]{0:T(128)S(1)} %get-tuple-element.62) | copy-start | bytes 772
  208.5 13.9 %copy-start.68 = (s32[64]{0:T(128)S(1)}, s32[64]{0:T(128)}, u32[]{:S(2)}) copy-start(s32[64]{0:T(128)} %copy-done.67) | copy-start | bytes 772
  208.5 13.9 %copy-start.78 = (f32[64]{0:T(128)S(1)}, f32[64]{0:T(128)}, u32[]{:S(2)}) copy-start(f32[64]{0:T(128)} %copy-done.77) | copy-start | bytes 772
  208.5 13.9 %copy-start.81 = (f32[64]{0:T(128)S(1)}, f32[64]{0:T(128)}, u32[]{:S(2)}) copy-start(f32[64]{0:T(128)} %copy-done.80) | copy-start | bytes 772
  231.0 22.5 %copy-start.13 = (bf16[64,5380]{1,0:T(8,128)(2,1)S(1)}, bf16[64,5380]{1,0:T(8,128)(2,1)}, u32[]{:S(2)}) copy-start(bf16[64,5380]{1,0:T(8,128)(2,1)} %constant_dynamic-update-slice_fusion.6) | copy-start | bytes 2065924
  231.4 22.1 %copy-start.48 = (f32[768]{0:T(1024)S(1)}, f32[768]{0:T(1024)}, u32[]{:S(2)}) copy-start(f32[768]{0:T(1024)} %copy-done.47) | copy-start | bytes 9220
  231.4 22.1 %copy-start.97 = (f32[64]{0:T(128)S(1)}, f32[64]{0:T(128)}, u32[]{:S(2)}) copy-start(f32[64]{0:T(128)} %copy-done.96) | copy-start | bytes 772
  231.4 33.3 %collective-permute-start.10 = (bf16[384,768]{1,0:T(8,128)(2,1)}, bf16[384,768]{1,0:T(8,128)(2,1)}, u32[]{:S(2)}, u32[]{:S(2)}) collective-permute-start(bf16[384,768]{1,0:T(8,128)(2,1)} %get-tuple-element.83), channel_id=1, source_target_pairs={{0,16},{16,0},{1,17},{17,1},{2,18},{18,2},{3,19},{19,3},{4,20},{20... | collective-permute-start | bytes 1769480 | tf_op jit(solution)/shard_map/ppermute | solution.py:550
  252.2 12.6 %collective-permute-start.9 = (bf16[384,768]{1,0:T(8,128)(2,1)}, bf16[384,768]{1,0:T(8,128)(2,1)}, u32[]{:S(2)}, u32[]{:S(2)}) collective-permute-start(bf16[384,768]{1,0:T(8,128)(2,1)} %get-tuple-element.79), channel_id=1, source_target_pairs={{0,16},{16,0},{1,17},{17,1},{2,18},{18,2},{3,19},{19,3},{4,20},{20... | collective-permute-start | bytes 1769480 | tf_op jit(solution)/shard_map/ppermute | solution.py:550
  252.2 16.4 %collective-permute-start.7 = (bf16[384,768]{1,0:T(8,128)(2,1)}, bf16[384,768]{1,0:T(8,128)(2,1)}, u32[]{:S(2)}, u32[]{:S(2)}) collective-permute-start(bf16[384,768]{1,0:T(8,128)(2,1)} %get-tuple-element.87), channel_id=1, source_target_pairs={{0,16},{16,0},{1,17},{17,1},{2,18},{18,2},{3,19},{19,3},{4,20},{20... | collective-permute-start | bytes 1769480 | tf_op jit(solution)/shard_map/ppermute | solution.py:550
  252.7 16.0 %collective-permute-start.8 = (bf16[384,768]{1,0:T(8,128)(2,1)}, bf16[384,768]{1,0:T(8,128)(2,1)}, u32[]{:S(2)}, u32[]{:S(2)}) collective-permute-start(bf16[384,768]{1,0:T(8,128)(2,1)} %get-tuple-element.85), channel_id=1, source_target_pairs={{0,16},{16,0},{1,17},{17,1},{2,18},{18,2},{3,19},{19,3},{4,20},{20... | collective-permute-start | bytes 1769480 | tf_op jit(solution)/shard_map/ppermute | solution.py:550
  259.3 1.6 collective-permute-start.6
  260.9 1.4 collective-permute-start.3
  262.3 1.4 collective-permute-start.4
  263.8 8.7 %collective-permute-start.5 = (bf16[64,5380]{1,0:T(8,128)(2,1)S(1)}, bf16[64,5380]{1,0:T(8,128)(2,1)S(1)}, u32[]{:S(2)}, u32[]{:S(2)}) collective-permute-start(bf16[64,5380]{1,0:T(8,128)(2,1)S(1)} %copy-done.22), channel_id=1, source_target_pairs={{0,16},{16,0},{1,17},{17,1},{2,18},{18,2},{3,19},{19,3},{4,20},{20... | collective-permute-start | bytes 2065928 | tf_op jit(solution)/shard_map/ppermute | solution.py:550
  (86 other events, 251.1 us)
